TPU v7x, 32 devices: a whole 2x2x4 slice. The times are simulated.
32 devices in a mesh: dp: 16 (over z, y, core), mp: 2 (over x).
Axes of the slice: x: 2, y: 2, z: 4, core: 2. Of those that a mesh axis runs over, the one named last changes fastest.
Arguments:
- tokens: bfloat16 [24576, 768], P('dp'), may hold values from -6 to 6
- out_grad: bfloat16 [24576, 768], P('dp'), may hold values from -6 to 6
- doc_lengths: int32 [16, 4], P('dp'), may hold values from 1 to 1024, 1536 in all within a row
- w_query: float32 [768, 768], P('dp', 'mp'), may hold values from -0.21875 to 0.21875
- w_key: float32 [768, 768], P('dp', 'mp'), may hold values from -0.21875 to 0.21875
- w_value: float32 [768, 768], P('dp', 'mp'), may hold values from -0.21875 to 0.21875
- w_out: float32 [768, 768], P('mp', 'dp'), may hold values from -0.875 to 0.875
- gain_one: float32 [768], P('dp'), may hold values from 0.5 to 1.5
- w_gate: float32 [768, 2560], P('dp', 'mp'), may hold values from -0.21875 to 0.21875
- w_up: float32 [768, 2560], P('dp', 'mp'), may hold values from -0.21875 to 0.21875
- w_down: float32 [2560, 768], P('mp', 'dp'), may hold values from -0.125 to 0.125
- gain_two: float32 [768], P('dp'), may hold values from 0.5 to 1.5
Outputs:
- output: bfloat16 [24576, 768], P('dp')
- grad_tokens: float32 [24576, 768], P('dp')
- grad_w_query: float32 [768, 768], P('dp', 'mp')
- grad_w_key: float32 [768, 768], P('dp', 'mp')
- grad_w_value: float32 [768, 768], P('dp', 'mp')
- grad_w_out: float32 [768, 768], P('mp', 'dp')
- grad_gain_one: float32 [768], P('dp')
- grad_w_gate: float32 [768, 2560], P('dp', 'mp')
- grad_w_up: float32 [768, 2560], P('dp', 'mp')
- grad_w_down: float32 [2560, 768], P('mp', 'dp')
- grad_gain_two: float32 [768], P('dp')
Inputs may be any that keep to these rules, and one draw needn't show every extreme that they name: `doc_lengths`: each row lists the lengths of the 4 documents packed into one pack of 1536 tokens, in order; they sum to 1536 and the largest is exactly 1024.
All inputs are finite; a program needn't handle non-finite values.
Results may differ from a plain program's by a relative error of at most 0.019.
The roundings to bfloat16 on the way count: a program that leaves them out, or rounds other values in their place, can miss the bound.
Values may be sent and summed in bfloat16 or wider, within the bound.
A program may use at most 256 MiB of HBM per device.

v0:
```python
import functools
import math
import jax, jax.numpy as jnp
from jax import lax
from jax.experimental import pallas as pl
from jax.experimental.pallas import tpu as pltpu
from jax.sharding import Mesh, PartitionSpec as P
MESH=pl.DeviceIdType.MESH
HD=48
C2=HD**-0.5*math.log2(math.e)
NEG=-1e30
bf=jnp.bfloat16; f32=jnp.float32
QB=256; LOOK=4
NT=(((1,),(1,)),((),()))
def dot(a,b): return jnp.dot(a,b,preferred_element_type=f32)
def dot_nt(a,b): return lax.dot_general(a,b,NT,preferred_element_type=f32)

def spread(rows, cols, rot):
    r=lax.broadcasted_iota(jnp.int32,(rows,cols),0); c=lax.broadcasted_iota(jnp.int32,(rows,cols),1)
    h=r//64; d=r-h*64
    if not rot:
        return jnp.where((d<HD)&(c==h*HD+d),1.0,0.0).astype(bf)
    lo=(d<24)&(c==h*HD+d+24); hi=(d>=24)&(d<HD)&(c==h*HD+d-24)
    return jnp.where(lo,-1.0,jnp.where(hi,1.0,0.0)).astype(bf)

def proj(tok,w,cos,sin,wq_s,q_s,k_s,v_s,n,cols):
    hp=cols//HD*64
    pairs=hp//128
    for m,(col,rot) in enumerate(((0,False),(0,True),(1,False),(1,True),(2,False))):
        if len(w.shape)==2:
            part=w[:,col*cols:(col+1)*cols]
        else:
            part=w[:,:,:,:,col*cols:(col+1)*cols].reshape(-1,cols)
        wq_s[m]=dot_nt(spread(hp,cols,rot),part).astype(bf)
    def body(b,_):
        rows=pl.ds(pl.multiple_of(b*QB,QB),QB)
        x=tok[rows,:]
        cs=cos[rows,:]; sn=sin[rows,:]
        for dst,a in ((q_s,0),(k_s,2)):
            raw=dot_nt(x,wq_s[a]); rt=dot_nt(x,wq_s[a+1])
            for p in range(pairs):
                l=slice(p*128,p*128+128)
                dst[p,rows,:]=(raw[:,l]*cs+rt[:,l]*sn).astype(bf)
        raw=dot_nt(x,wq_s[4])
        for p in range(pairs):
            v_s[p,rows,:]=raw[:,p*128:p*128+128].astype(bf)
        return 0
    lax.fori_loop(0,n//QB,body,0)

def masks(kk0,nk,i,start):
    kidx=lax.broadcasted_iota(jnp.int32,(nk,QB),0)+kk0
    ok=kidx>=start
    qidx=lax.broadcasted_iota(jnp.int32,(nk,QB),1)+i*QB
    return ok&(kidx<=qidx)

def fwd_head(h,i,q_t,k_s,v_t,start,m_t,lse):
    p=h//2; half=h-2*p
    lo=max(0,i-LOOK)*QB; nk=(i+1)*QB-lo
    kk=slice(lo,lo+nk); qq=slice(i*QB,(i+1)*QB)
    row=lax.broadcasted_iota(jnp.int32,(128,QB),0)
    mine=(row>=half*64)&(row<half*64+64)
    qt=jnp.where(mine,q_t[p,:,qq],jnp.zeros((),bf))
    s=dot(k_s[p,kk,:],qt)
    st=start[:,qq]
    s=jnp.where(masks(lo,nk,i,st),s,NEG)
    m=jnp.max(s,0,keepdims=True)
    e=jnp.exp2((s-m)*C2)
    l=jnp.sum(e,0,keepdims=True)
    pr=(e*(1.0/l)).astype(bf)
    rows=pl.ds(pl.multiple_of(half*64,64),64)
    m_t[p,rows,qq]=dot(v_t[p,rows,kk],pr)
    lse[pl.ds(h,1),qq]=m*C2+jnp.log2(l)

def fwd_kernel(n,cols,tok,w,cos,sin,start,q_o,k_o,v_o,m_t,mixed,lse,wq_s,q_t,v_t):
    proj(tok,w,cos,sin,wq_s,q_o,k_o,v_o,n,cols)
    heads=cols//HD
    for p in range(heads//2):
        q_t[p]=q_o[p].T
        v_t[p]=v_o[p].T
    def body(h,_):
        for i in range(n//QB):
            fwd_head(h,i,q_t,k_o,v_t,start,m_t,lse)
        return 0
    lax.fori_loop(0,heads,body,0)
    for p in range(heads//2):
        mixed[:,p*128:p*128+128]=m_t[p].T.astype(bf)

def attn_fwd(tok,w,cos,sin,start):
    n=tok.shape[0]; cols=w.shape[1]//3; heads=cols//HD; P=heads//2
    V=pl.BlockSpec(memory_space=pltpu.VMEM)
    S=jax.ShapeDtypeStruct
    return pl.pallas_call(functools.partial(fwd_kernel,n,cols),
      out_shape=(S((P,n,128),bf),S((P,n,128),bf),S((P,n,128),bf),S((P,128,n),f32),S((n,P*128),bf),S((heads,n),f32)),
      in_specs=[V]*5,out_specs=[V]*6,
      scratch_shapes=[pltpu.VMEM((5,P*128,w.shape[0]),bf),pltpu.VMEM((P,128,n),bf),pltpu.VMEM((P,128,n),bf)],
      compiler_params=pltpu.CompilerParams(vmem_limit_bytes=60<<20),name="attn_fwd")(tok,w,cos,sin,start)

def bwd_head(h,i,q_t,q_s,k_s,k_t,v_s,dm_t,dm_s,lse,dd,start,dq_t,dk_s,dv_s):
    p=h//2; half=h-2*p
    lo=max(0,i-LOOK)*QB; nk=(i+1)*QB-lo
    kk=slice(lo,lo+nk); qq=slice(i*QB,(i+1)*QB)
    row=lax.broadcasted_iota(jnp.int32,(128,QB),0)
    mine=(row>=half*64)&(row<half*64+64)
    lane=lax.broadcasted_iota(jnp.int32,(QB,128),1)
    mlane=(lane>=half*64)&(lane<half*64+64)
    zero=jnp.zeros((),bf)
    qt=jnp.where(mine,q_t[p,:,qq],zero)
    dmt=jnp.where(mine,dm_t[p,:,qq],zero)
    qn=jnp.where(mlane,q_s[p,qq,:],zero)
    dmn=jnp.where(mlane,dm_s[p,qq,:],zero)
    s=dot(k_s[p,kk,:],qt)
    st=start[:,qq]
    pr=jnp.exp2(jnp.where(masks(lo,nk,i,st),s*C2,NEG)-lse[pl.ds(h,1),qq])
    dp=dot(v_s[p,kk,:],dmt)
    ds=(pr*(dp-dd[pl.ds(h,1),qq])).astype(bf)
    pb=pr.astype(bf)
    dv_s[p,kk,:]+=dot(pb,dmn)
    dk_s[p,kk,:]+=dot(ds,qn)
    rows=pl.ds(pl.multiple_of(half*64,64),64)
    dq_t[p,rows,qq]=dot(k_t[p,rows,kk],ds)

def rope_back(u,cs,sn):
    w=u*sn
    lane=lax.broadcasted_iota(jnp.int32,u.shape,1)&63
    up=pltpu.roll(w,128-24,axis=1); dn=pltpu.roll(w,24,axis=1)
    return u*cs+jnp.where(lane<24,up,jnp.where(lane<48,-dn,0.0))

def bwd_kernel(n,heads,q_s,k_s,v_s,m_t,dm,lse,start,cos,sin,dqkv,q_t,k_t,dm_t,dm_s,dq_t,dk_s,dv_s,dd):
    P=heads//2
    for p in range(P):
        q_t[p]=q_s[p].T
        k_t[p]=k_s[p].T
        dm_s[p]=dm[:,p*128:p*128+128]
        dm_t[p]=dm_s[p].T
        for half in range(2):
            r=slice(half*64,half*64+64)
            dd[2*p+half:2*p+half+1,:]=jnp.sum(dm_t[p,r,:].astype(f32)*m_t[p,r,:],0,keepdims=True)
    dk_s[...]=jnp.zeros_like(dk_s); dv_s[...]=jnp.zeros_like(dv_s)
    def body(h,_):
        for i in range(n//QB):
            bwd_head(h,i,q_t,q_s,k_s,k_t,v_s,dm_t,dm_s,lse,dd,start,dq_t,dk_s,dv_s)
        return 0
    lax.fori_loop(0,heads,body,0)
    sc=HD**-0.5
    for p in range(P):
        dqkv[0,:,p*128:p*128+128]=rope_back(dq_t[p].T*sc,cos[...],sin[...]).astype(bf)
        dqkv[1,:,p*128:p*128+128]=rope_back(dk_s[p]*sc,cos[...],sin[...]).astype(bf)
        dqkv[2,:,p*128:p*128+128]=dv_s[p].astype(bf)

def attn_bwd(q_s,k_s,v_s,m_t,dm,lse,start,cos,sin):
    P,n,_=q_s.shape; heads=2*P
    V=pl.BlockSpec(memory_space=pltpu.VMEM)
    S=jax.ShapeDtypeStruct
    return pl.pallas_call(functools.partial(bwd_kernel,n,heads),
      out_shape=S((3,n,P*128),bf),
      in_specs=[V]*9,out_specs=V,
      scratch_shapes=[pltpu.VMEM((P,128,n),bf),pltpu.VMEM((P,128,n),bf),pltpu.VMEM((P,128,n),bf),pltpu.VMEM((P,n,128),bf),pltpu.VMEM((P,128,n),f32),pltpu.VMEM((P,n,128),f32),pltpu.VMEM((P,n,128),f32),pltpu.VMEM((heads,n),f32)],
      compiler_params=pltpu.CompilerParams(vmem_limit_bytes=60<<20),name="attn_bwd")(q_s,k_s,v_s,m_t,dm,lse,start,cos,sin)


def place():
    q,m=lax.axis_index("q"),lax.axis_index("m")
    return q//2,lax.rem(q,2),m

def peers(z,y,m):
    return [{"q":z*2+1-y},{"m":1-m}]+[{"q":lax.rem(z+s,4)*2+y} for s in (1,2,3)]

def greet(where):
    barrier=pltpu.get_barrier_semaphore()
    for w in where:
        pl.semaphore_signal(barrier,inc=1,device_id=w,device_id_type=MESH)
    pl.semaphore_wait(barrier,len(where))

class Halve:
    def __init__(self,source,one,two,send,recv,first):
        self.source,self.one,self.two,self.first=source,one,two,first
        z,y,m=place()
        self.y,self.m=y,m
        to=peers(z,y,m)
        a,b=(0,1) if first=="y" else (1,0)
        copy=lambda s,d,k,w: pltpu.make_async_remote_copy(src_ref=s,dst_ref=d,send_sem=send.at[k],recv_sem=recv.at[k],device_id=w,device_id_type=MESH)
        self.c1=copy(source.at[:,1-y] if first=="y" else source.at[:,:,1-m],one,0,to[a])
        self.c2=copy(one.at[:,(1-m) if first=="y" else (1-y)],two,1,to[b])
    def start(self):
        self.c1.start()
    def second(self):
        self.c1.wait_recv()
        def add(i,_):
            zz=i//2; o=i-zz*2
            mine=self.source[zz,self.y,o] if self.first=="y" else self.source[zz,o,self.m]
            self.one[zz,o]=(self.one[zz,o].astype(f32)+mine.astype(f32)).astype(bf)
            return 0
        lax.fori_loop(0,8,add,0)
        self.c2.start()
    def third(self):
        self.c2.wait_recv()
        keep=self.m if self.first=="y" else self.y
        def add(zz,_):
            self.two[zz]=(self.two[zz].astype(f32)+self.one[zz,keep].astype(f32)).astype(bf)
            return 0
        lax.fori_loop(0,4,add,0)
    def drain(self):
        self.c1.wait_send(); self.c2.wait_send()

class Quarter:
    def __init__(self,two,three,out,send,recv):
        self.two,self.three,self.out=two,three,out
        z,y,m=place()
        self.z=z
        to=peers(z,y,m)
        self.c3=[pltpu.make_async_remote_copy(src_ref=two.at[lax.rem(z+s,4)],dst_ref=three.at[s-1],send_sem=send.at[s-1],recv_sem=recv.at[s-1],
            device_id=to[1+s],device_id_type=MESH) for s in (1,2,3)]
    def start(self):
        for c in self.c3: c.start()
    def finish(self):
        for c in self.c3: c.wait_recv()
        t=self.two[self.z].astype(f32)
        for s in range(3): t=t+self.three[s].astype(f32)
        self.out[...]=t.astype(bf)
    def drain(self):
        for c in self.c3: c.wait_send()

def halve_scratch(c):
    return [pltpu.VMEM((4,2,48,c),bf),pltpu.SemaphoreType.DMA((2,)),pltpu.SemaphoreType.DMA((2,))]
def quarter_scratch(c):
    return [pltpu.VMEM((3,48,c),bf),pltpu.SemaphoreType.DMA((3,)),pltpu.SemaphoreType.DMA((3,))]


class Gather:
    def __init__(self,full,cols,send,recv,first):
        z,y,m=place()
        to=peers(z,y,m)
        a,b=(0,1) if first=="y" else (1,0)
        def copy(at,k,w):
            return pltpu.make_async_remote_copy(src_ref=at,dst_ref=at,send_sem=send.at[k],recv_sem=recv.at[k],device_id=w,device_id_type=MESH)
        self.along=[copy(full.at[z,y,m,:,cols],s-1,to[1+s]) for s in (1,2,3)]
        self.c2=copy(full.at[:,y,m,:,cols],3,to[a])
        self.c3=copy(full.at[:,:,m,:,cols] if first=="y" else full.at[:,y,:,:,cols],4,to[b])
    def start(self):
        for c in self.along: c.start()
    def second(self):
        for c in self.along: c.wait_recv()
        self.c2.start()
    def third(self):
        self.c2.wait_recv()
        self.c3.start()
    def finish(self):
        self.c3.wait_recv()
    def drain(self):
        for c in self.along: c.wait_send()
        self.c2.wait_send(); self.c3.wait_send()

def both(c,m):
    return [{"c":1-c},{"c":1-c,"m":1-m}]

def fused_fwd_kernel(n,cols,ff,tok_i,og_i,cos_i,sin_i,start_i,a_i,o_i,g_i,u_i,d_i,
        tok,og,cos,sin,start,wa,wo,wg,wu,wd,q_o,k_o,v_o,m_t,mixed,lse,tok_t,wt,
        wq_s,q_t,v_t,swap_s,swap_r,put_s,put_r,*sems):
    z,y,m=place(); c=lax.axis_index("c")
    own=c==m
    greet(peers(z,y,m)+both(c,m))
    def remote(s,d,ss,rs,w):
        return pltpu.make_async_remote_copy(src_ref=s,dst_ref=d,send_sem=ss,recv_sem=rs,device_id=w,device_id_type=MESH)
    diag={"c":1-c,"m":1-m}
    shards=[(a_i,wa),(g_i,wg),(u_i,wu),(d_i,wd),(o_i,wo)]
    put_far=[remote(s,d.at[z,y,c],put_s.at[i],put_r.at[i],diag) for i,(s,d) in enumerate(shards)]
    put_near=[pltpu.make_async_copy(s,d.at[z,y,c],put_r.at[i]) for i,(s,d) in enumerate(shards)]
    packs=[(tok_i,tok),(cos_i,cos),(sin_i,sin),(start_i,start),(og_i,og)]
    swap_far=[remote(s,d,swap_s.at[i],swap_r.at[i],{"c":1-c}) for i,(s,d) in enumerate(packs)]
    swap_near=[pltpu.make_async_copy(s,d,swap_r.at[i]) for i,(s,d) in enumerate(packs)]
    @pl.when(own)
    def _():
        for x in put_near: x.start()
        for a,b in zip(swap_near,swap_far):
            a.start(); b.start()
        put_near[0].wait()
    @pl.when(jnp.logical_not(own))
    def _():
        for x in put_far: x.start()
        put_far[0].wait_recv()
    def ga(full,lo,hi,k,first): return Gather(full,slice(lo,hi),sems[2*k],sems[2*k+1],first)
    ac=wa.shape[-1]; cut=[0,ac//1280*256,ac//2,ac//2+ac//1280*384,ac]
    a=[ga(wa,cut[i],cut[i+1],i,"xy"[i%2]) for i in range(4)]
    h2=ff//2
    f=[ga(w,j*h2,j*h2+h2,4+2*i+j,"xy"[j]) for i,w in enumerate((wg,wu,wd)) for j in range(2)]
    f.append(ga(wo,0,wo.shape[-1],10,"x"))
    for x in a: x.start()
    @pl.when(own)
    def _():
        for x in put_near[1:]: x.wait()
    @pl.when(jnp.logical_not(own))
    def _():
        for x in put_far[1:]: x.wait_recv()
    a[0].second(); a[1].second()
    for x in f: x.start()
    @pl.when(own)
    def _():
        for x in swap_near: x.wait()
    @pl.when(jnp.logical_not(own))
    def _():
        for x in swap_far: x.wait_recv()
    a[0].third(); a[1].third()
    a[2].second(); a[3].second()
    tok_t[:tok_t.shape[0]//2,:]=tok[:,:tok_t.shape[0]//2].T
    a[2].third(); a[3].third()
    tok_t[tok_t.shape[0]//2:,:]=tok[:,tok_t.shape[0]//2:].T
    for x in a: x.finish()
    f[0].second(); f[1].second()
    proj(tok,wa,cos,sin,wq_s,q_o,k_o,v_o,n,cols)
    f[0].third(); f[1].third()
    f[2].second(); f[3].second()
    for j in range(3): wt[j]=wq_s[2*j]
    heads=cols//HD
    for p in range(heads//2):
        q_t[p]=q_o[p].T
        v_t[p]=v_o[p].T
    plan={1:[(4,"second"),(5,"second")],2:[(2,"third"),(3,"third")],3:[(6,"second")],4:[(4,"third"),(5,"third")],5:[(6,"third")]}
    def body(h,_):
        for i in range(n//QB):
            fwd_head(h,i,q_t,k_o,v_t,start,m_t,lse)
        for at,todo in plan.items():
            @pl.when(h==at)
            def _():
                for k,what in todo: getattr(f[k],what)()
        return 0
    lax.fori_loop(0,heads,body,0)
    for p in range(heads//2):
        mixed[:,p*128:p*128+128]=m_t[p].T.astype(bf)
    for x in f: x.finish()
    for x in a+f: x.drain()
    @pl.when(own)
    def _():
        for x in swap_far: x.wait_send()
    @pl.when(jnp.logical_not(own))
    def _():
        for x in put_far: x.wait_send()

def fused_fwd(tok,og,cos,sin,start,a,o,g,u,d,cols):
    n,width=tok.shape; heads=cols//HD; pr=heads//2; ff=g.shape[1]
    V=pl.BlockSpec(memory_space=pltpu.VMEM); A=pl.BlockSpec(memory_space=pl.ANY)
    S=jax.ShapeDtypeStruct
    like=lambda a: S(a.shape,a.dtype)
    wide=lambda a: S((4,2,2)+a.shape,bf)
    dma=lambda k: pltpu.SemaphoreType.DMA((k,))
    return pl.pallas_call(functools.partial(fused_fwd_kernel,n,cols,ff),
      out_shape=[like(tok),like(og),like(cos),like(sin),like(start),wide(a),wide(o),wide(g),wide(u),wide(d),
        S((pr,n,128),bf),S((pr,n,128),bf),S((pr,n,128),bf),S((pr,128,n),f32),S((n,pr*128),bf),S((heads,n),f32),S((width,n),bf),S((3,pr*128,width),bf)],
      in_specs=[A]*10,out_specs=[V]*18,
      scratch_shapes=[pltpu.VMEM((5,pr*128,width),bf),pltpu.VMEM((pr,128,n),bf),pltpu.VMEM((pr,128,n),bf),
        dma(5),dma(5),dma(5),dma(5)]+[dma(5)]*22,
      compiler_params=pltpu.CompilerParams(vmem_limit_bytes=60<<20,collective_id=0,has_side_effects=True),name="attn_fwd_gather")(tok,og,cos,sin,start,a,o,g,u,d)

def fused_bwd_kernel(n,heads,q_s,k_s,v_s,m_t,dm,lse,start,cos,sin,gg,gu,gd,dqkv,t0,t1,t2,t3,t4,t5,q_t,k_t,dm_t,dm_s,dq_t,dk_s,dv_s,dd,*scr):
    z,y,m=place()
    greet(peers(z,y,m))
    half=gg.shape[-1]//2
    two=[t0,t1,t2,t3,t4,t5]
    ch=[]
    for k in range(6):
        src=(gd,gg,gu)[k//2]
        one,s,r=scr[3*k:3*k+3]
        ch.append(Halve(src.at[:,:,:,:,(k%2)*half:(k%2)*half+half],one,two[k],s,r,"yx"[k%2]))
    for x in ch: x.start()
    P_=heads//2
    for p in range(P_):
        q_t[p]=q_s[p].T
        k_t[p]=k_s[p].T
        dm_s[p]=dm[:,p*128:p*128+128]
        dm_t[p]=dm_s[p].T
        for half_ in range(2):
            r=slice(half_*64,half_*64+64)
            dd[2*p+half_:2*p+half_+1,:]=jnp.sum(dm_t[p,r,:].astype(f32)*m_t[p,r,:],0,keepdims=True)
    dk_s[...]=jnp.zeros_like(dk_s); dv_s[...]=jnp.zeros_like(dv_s)
    plan={1:[(0,"second"),(1,"second")],3:[(0,"third"),(1,"third")],4:[(2,"second"),(3,"second")],6:[(2,"third"),(3,"third")],7:[(4,"second"),(5,"second")]}
    def body(h,_):
        for i in range(n//QB):
            bwd_head(h,i,q_t,q_s,k_s,k_t,v_s,dm_t,dm_s,lse,dd,start,dq_t,dk_s,dv_s)
        for at,todo in plan.items():
            @pl.when(h==at)
            def _():
                for k,what in todo: getattr(ch[k],what)()
        return 0
    lax.fori_loop(0,heads,body,0)
    sc=HD**-0.5
    for p in range(P_):
        dqkv[0,:,p*128:p*128+128]=rope_back(dq_t[p].T*sc,cos[...],sin[...]).astype(bf)
        dqkv[1,:,p*128:p*128+128]=rope_back(dk_s[p]*sc,cos[...],sin[...]).astype(bf)
        dqkv[2,:,p*128:p*128+128]=dv_s[p].astype(bf)
    ch[4].third(); ch[5].third()
    for x in ch: x.drain()

def fused_bwd(q_s,k_s,v_s,m_t,dm,lse,start,cos,sin,gg,gu,gd):
    pr,n,_=q_s.shape; heads=2*pr
    V=pl.BlockSpec(memory_space=pltpu.VMEM)
    S=jax.ShapeDtypeStruct
    ff=gg.shape[1]
    cut=lambda a: a.reshape(4,2,2,48,ff)
    return pl.pallas_call(functools.partial(fused_bwd_kernel,n,heads),
      out_shape=[S((3,n,pr*128),bf)]+[S((4,48,ff//2),bf)]*6,
      in_specs=[V]*12,out_specs=[V]*7,
      scratch_shapes=[pltpu.VMEM((pr,128,n),bf),pltpu.VMEM((pr,128,n),bf),pltpu.VMEM((pr,128,n),bf),pltpu.VMEM((pr,n,128),bf),pltpu.VMEM((pr,128,n),f32),pltpu.VMEM((pr,n,128),f32),pltpu.VMEM((pr,n,128),f32),pltpu.VMEM((heads,n),f32)]
        +sum([halve_scratch(ff//2) for _ in range(6)],[]),
      compiler_params=pltpu.CompilerParams(vmem_limit_bytes=60<<20,collective_id=1,has_side_effects=True),name="attn_bwd_reduce")(
        q_s,k_s,v_s,m_t,dm,lse,start,cos,sin,cut(gg),cut(gu),cut(gd))

def tail_kernel(n,cols,dqkv,tok_t,wt,dattn,mixed,d_one,gains,t0,t1,t2,t3,t4,t5,og,ou,od,oa,gtok,ga,term,other,summed,core_s,core_r,far_s,far_r,
        h0,h0s,h0r,h1,h1s,h1r,two0,two1,*scr):
    z,y,m=place(); c=lax.axis_index("c")
    own=c==m
    greet(peers(z,y,m)+both(c,m))
    half=t0.shape[-1]
    ff=[]
    for k,t in enumerate((t0,t1,t2,t3,t4,t5)):
        three,s,r=scr[3*k:3*k+3]
        ff.append(Quarter(t,three,(od,og,ou)[k//2].at[:,(k%2)*half:(k%2)*half+half],s,r))
    for x in ff: x.start()
    w=ga.shape[-1]; mid=2*cols+128
    c0,c1=ga.at[:,:,:,:,0:mid],ga.at[:,:,:,:,mid:w]
    halves=[Halve(c0,h0,two0,h0s,h0r,"y"),Halve(c1,h1,two1,h1s,h1r,"y")]
    quarters=[Quarter(two0,scr[18],oa.at[:,0:mid],scr[19],scr[20]),Quarter(two1,scr[21],oa.at[:,mid:w],scr[22],scr[23])]
    put=spread(cols//HD*64,cols,False)
    width=tok_t.shape[0]; part=width//2
    def pack(val): return val.reshape(2,2,2,48,val.shape[-1])
    for i in range(2):
        zz=slice(2*i,2*i+2); rows=slice(i*part,(i+1)*part)
        ga[zz,:,:,:,0:128]=pack(gains[rows,:])
        ga[zz,:,:,:,128:128+cols]=pack(dot_nt_t(dattn[:,rows].T,mixed[...],put))
        ga[zz,:,:,:,128+cols:128+2*cols]=pack(dot_nt_t(tok_t[rows,:],dqkv[0],put))
    halves[0].start()
    for i in range(2):
        zz=slice(2*i,2*i+2); rows=slice(i*part,(i+1)*part)
        for j in (1,2):
            ga[zz,:,:,:,128+(j+1)*cols:128+(j+2)*cols]=pack(dot_nt_t(tok_t[rows,:],dqkv[j],put))
    halves[1].start()
    nb=n//QB
    def cross(b): return pltpu.make_async_remote_copy(src_ref=term.at[b],dst_ref=other.at[b],send_sem=core_s.at[b],recv_sem=core_r.at[b],device_id={"c":1-c},device_id_type=MESH)
    def far(b): return pltpu.make_async_remote_copy(src_ref=summed.at[b],dst_ref=gtok.at[b],send_sem=far_s.at[b],recv_sem=far_r.at[b],device_id={"c":1-c,"m":1-m},device_id_type=MESH)
    def near(b): return pltpu.make_async_copy(summed.at[b],gtok.at[b],far_r.at[b])
    def make(b,_):
        rows=pl.ds(pl.multiple_of(b*QB,QB),QB)
        t=dot(dqkv[0,rows,:],wt[0])+dot(dqkv[1,rows,:],wt[1])+dot(dqkv[2,rows,:],wt[2])
        term[b]=t.astype(bf)
        cross(b).start()
        return 0
    lax.fori_loop(0,nb,make,0)
    def total(b,_):
        rows=pl.ds(pl.multiple_of(b*QB,QB),QB)
        cross(b).wait_recv()
        summed[b]=(d_one[rows,:]+(term[b].astype(f32)+other[b].astype(f32))).astype(bf)
        @pl.when(own)
        def _():
            near(b).start()
        @pl.when(jnp.logical_not(own))
        def _():
            far(b).start()
        return 0
    lax.fori_loop(0,nb,total,0)
    halves[0].second()
    for x in ff[:2]: x.finish()
    halves[1].second()
    for x in ff[2:]: x.finish()
    halves[0].third(); quarters[0].start()
    halves[1].third(); quarters[1].start()
    quarters[0].finish(); quarters[1].finish()
    for x in ff+halves+quarters: x.drain()
    def drain(b,_):
        cross(b).wait_send()
        @pl.when(own)
        def _():
            near(b).wait()
        @pl.when(jnp.logical_not(own))
        def _():
            far(b).wait_recv()
            far(b).wait_send()
        return 0
    lax.fori_loop(0,nb,drain,0)

def dot_nt_t(a,b,put):
    return dot(dot(a,b).astype(bf),put).astype(bf)

def tail(dqkv,tok_t,wt,dattn,mixed,d_one,gains,twos,cols):
    n,width=dattn.shape; ff=2*twos[0].shape[-1]; w=4*cols+128; mid=2*cols+128
    V=pl.BlockSpec(memory_space=pltpu.VMEM); A=pl.BlockSpec(memory_space=pl.ANY)
    S=jax.ShapeDtypeStruct
    blocks=(n//QB,QB,width)
    dma=lambda k: pltpu.SemaphoreType.DMA((k,))
    half=lambda k: [pltpu.VMEM((4,2,48,k),bf),dma(2),dma(2)]
    return pl.pallas_call(functools.partial(tail_kernel,n,cols),
      out_shape=[S((48,ff),bf)]*3+[S((48,w),bf),S(blocks,bf)],
      in_specs=[V]*13,out_specs=[V]*4+[A],
      scratch_shapes=[pltpu.VMEM((4,2,2,48,w),bf),pltpu.VMEM(blocks,bf),pltpu.VMEM(blocks,bf),pltpu.VMEM(blocks,bf)]+[dma(n//QB)]*4
        +halve_scratch(mid)+halve_scratch(w-mid)+[pltpu.VMEM((4,48,mid),bf),pltpu.VMEM((4,48,w-mid),bf)]
        +sum([quarter_scratch(ff//2) for _ in range(6)],[])+quarter_scratch(mid)+quarter_scratch(w-mid),
      compiler_params=pltpu.CompilerParams(vmem_limit_bytes=60<<20,collective_id=2,has_side_effects=True),name="token_grad_reduce")(
        dqkv,tok_t,wt,dattn,mixed,d_one,gains,*twos)

NORM_EPS=1e-05
DIAG=[(0,0),(3,3),(1,2),(2,1)]
CORE=[(0,1),(1,0)]

def rms_forward(resid):
    inverse=lax.rsqrt(jnp.mean(resid*resid,-1,keepdims=True)+NORM_EPS)
    return (resid*inverse,inverse)

def rms_backward(grad_normed,normed,inverse):
    return inverse*(grad_normed-normed*jnp.mean(grad_normed*normed,-1,keepdims=True))

def doc_starts(lengths,n):
    at=jnp.arange(n,dtype=jnp.int32); start=jnp.zeros((n,),jnp.int32); end=jnp.int32(0)
    for i in range(lengths.shape[0]-1):
        end=end+lengths[i]
        start=jnp.where(at>=end,end,start)
    return start

def rope_tables(positions):
    half=HD//2
    fr=jnp.exp(jnp.arange(half,dtype=f32)*(-2.0*math.log(10000.0)/HD))
    a=positions.astype(f32)[:,None]*fr[None,:]
    c,s=jnp.cos(a),jnp.sin(a); z=jnp.zeros((positions.shape[0],64-HD),f32)
    return jnp.concatenate([c,c,z,c,c,z],1),jnp.concatenate([s,s,z,s,s,z],1)

def core_sum(part):
    return part.astype(f32)+lax.ppermute(part,"c",CORE).astype(f32)

def on_device(tokens,out_grad,doc_lengths,w_query,w_key,w_value,w_out,gain_one,w_gate,w_up,w_down,gain_two):
    cols=w_query.shape[1]; ff=w_gate.shape[1]; n,width=tokens.shape
    quad=lax.axis_size("q")==8 and w_query.shape[0]==48
    if not quad:
        own=lax.axis_index("c")==lax.axis_index("m")
        pick=lambda a: jnp.where(own,a,lax.ppermute(a,"c",CORE))
        tokens,out_grad,doc_lengths=pick(tokens),pick(out_grad),pick(doc_lengths)
    start=doc_starts(doc_lengths[0],n)
    cos,sin=rope_tables(jnp.arange(n,dtype=jnp.int32)-start)
    start=start[None]
    cast=lambda a: a.astype(bf)
    gains=jnp.pad(jnp.stack([cast(gain_one),cast(gain_two)],1),((0,0),(0,126)))
    apack=jnp.concatenate([cast(w_query),cast(w_key),cast(w_value),gains],1)
    def gather(a):
        return lax.all_gather(lax.ppermute(a,("c","m"),DIAG),("q","m"),axis=0,tiled=True)
    if quad:
        tokens,out_grad,cos,sin,start,afull,ofull,gate_w,up_w,down_t,q,k,v,m_t,mixed,lse,tok_t,wt=fused_fwd(
            tokens,out_grad,cos,sin,start,apack,cast(w_out).T,cast(w_gate),cast(w_up),cast(w_down).T,cols)
        afull,ofull,gate_w,up_w,down_t=[a.reshape(width,a.shape[-1]) for a in (afull,ofull,gate_w,up_w,down_t)]
    else:
        afull,ofull,gate_w,up_w,down_t=[gather(a) for a in (apack,cast(w_out).T,cast(w_gate),cast(w_up),cast(w_down).T)]
        q,k,v,m_t,mixed,lse=attn_fwd(tokens,afull[:,:3*cols],cos,sin,start)
    hp=cols//HD*64
    put=spread(hp,cols,False)
    out_t=dot_nt(ofull,put).astype(bf)
    gain_a=afull[:,3*cols].astype(f32); gain_b=afull[:,3*cols+1].astype(f32)
    attn=core_sum(dot_nt(mixed,out_t).astype(bf))
    normed_one,inv_one=rms_forward(tokens.astype(f32)+attn)
    hidden=normed_one*gain_a
    hb=hidden.astype(bf)
    gate=dot(hb,gate_w); up=dot(hb,up_w)
    sg=jax.nn.sigmoid(gate)
    act=(gate*sg*up).astype(bf)
    ffn=core_sum(dot_nt(act,down_t).astype(bf))
    normed_two,inv_two=rms_forward(hidden+ffn)
    output=(normed_two*gain_b).astype(bf)
    g=out_grad.astype(f32)
    g_gain_two=jnp.sum(g*normed_two,0)
    d_two=rms_backward(g*gain_b,normed_two,inv_two)
    d_ffn=d_two.astype(bf)
    tn=lambda a,b: lax.dot_general(a,b,(((0,),(0,)),((),())),preferred_element_type=f32)
    d_act=dot(d_ffn,down_t)
    d_up=(d_act*gate*sg).astype(bf)
    d_gate=(d_act*up*sg*(1.0+gate*(1.0-sg))).astype(bf)
    hterm=(dot_nt(d_gate,gate_w)+dot_nt(d_up,up_w)).astype(bf)
    gff=[tn(hb,d_gate).astype(bf),tn(hb,d_up).astype(bf),tn(d_ffn,act).astype(bf)]
    d_hidden=d_two+core_sum(hterm)
    g_gain_one=jnp.sum(d_hidden*normed_one,0)
    d_one=rms_backward(d_hidden*gain_a,normed_one,inv_one)
    d_attn=d_one.astype(bf)
    dm=dot(d_attn,out_t).astype(bf)
    ggain=jnp.pad(jnp.stack([g_gain_one,g_gain_two],1),((0,0),(0,126))).astype(bf)
    own=lax.axis_index("c")==lax.axis_index("m")
    output=jnp.where(own,output,lax.ppermute(output,("c","m"),[(1,2),(2,1)]))
    if quad:
        dqkv,*twos=fused_bwd(q,k,v,m_t,dm,lse,start,cos,sin,*gff)
        *sff,sat,gtok=tail(dqkv,tok_t,wt,d_attn,mixed,d_one,ggain,twos,cols)
        gtok=gtok.reshape(n,width).astype(f32)
    else:
        dqkv=attn_bwd(q,k,v,m_t,dm,lse,start,cos,sin)
        term=0.0; gqkv=[]
        for j in range(3):
            wp=dot_nt(afull[:,j*cols:(j+1)*cols],put).astype(bf)
            term=term+dot_nt(dqkv[j],wp)
            gqkv.append(dot(tn(tokens,dqkv[j]).astype(bf),put).astype(bf))
        gtok=(d_one+core_sum(term.astype(bf))).astype(bf)
        gtok=lax.ppermute(gtok,("c","m"),DIAG).astype(f32)
        g_out=dot(tn(d_attn,mixed).astype(bf),put).astype(bf)
        gatt=jnp.concatenate([ggain,g_out]+gqkv,1)
        add=lambda a: lax.psum_scatter(a,("q","m"),scatter_dimension=0,tiled=True)
        sff,sat=[add(a) for a in gff],add(gatt)
    sff,sat=lax.ppermute(jnp.concatenate(sff,1),("c","m"),DIAG).astype(f32),lax.ppermute(sat,("c","m"),DIAG).astype(f32)
    piece=lambda j: sat[:,128+j*cols:128+(j+1)*cols]
    return (output,gtok,piece(1),piece(2),piece(3),piece(0).T,sat[:,0],sff[:,:ff],sff[:,ff:2*ff],sff[:,2*ff:].T,sat[:,1])

def solution(mesh):
    dp,mp=mesh.shape["dp"],mesh.shape["mp"]
    fine=Mesh(mesh.devices.reshape(dp//2,2,mp),("q","c","m"))
    d=("q","c")
    rows,cols_=P(d,"m"),P("m",d)
    return jax.shard_map(on_device,mesh=fine,
        in_specs=(P(d,None),P(d,None),P(d,None),rows,rows,rows,cols_,P(d),rows,rows,cols_,P(d)),
        out_specs=(P(d,None),P(d,None),rows,rows,rows,cols_,P(d),rows,rows,cols_,P(d)),check_vma=False)
```

profile of v0, /device:TPU:1, one launch (start us, length us, event | category | flops | bytes accessed | tf_op | source)
XLA Modules:
  0.0 373.0 jit_solution(15967126344977357213)
XLA Ops:
  5.9 2.8 multiply_sine_fusion
  8.7 3.0 concatenate.12.cos_i
  11.8 2.4 concatenate.13.sin_i
  17.7 107.0 %attn_fwd_gather.1 = (bf16[1536,768]{1,0:T(8,128)(2,1)}, bf16[1536,768]{1,0:T(8,128)(2,1)}, f32[1536,128]{1,0:T(8,128)}, f32[1536,128]{1,0:T(8,128)}, s32[1,1536...) custom-call(bf16[1536,768]{1,0:T(8,128)(2,1)} %tok_i.1, ...), custom_call_target="tpu_custom_call" | custom-call | tf_op jit(solution)/shard_map/attn_fwd_gather/pallas_call | solution.py:345
  124.7 1.9 convolution_convert_fusion.6
  126.6 4.4 %convolution_convert_fusion.4 = bf16[1536,768]{1,0:T(8,128)(2,1)} fusion(bf16[1536,512]{1,0:T(8,128)(2,1)} %get-tuple-element.42.mixed, bf16[768,512]{1,0:T(8,128)(2,1)S(1)} %convolution_convert_fusion.6), kind=kOutput, calls=%fused_computation.26 | convolution fusion | flops 1209139200 | bytes 4718592 | tf_op jit(solution)/shard_map/dot_general | solution.py:16
  132.3 3.6 collective-permute-done
  135.9 3.5 multiply_reduce_fusion.3
  139.9 2.5 copy-done.22
  142.4 3.2 fusion.34
  145.7 5.8 %multiply_convert_fusion.2 = (bf16[1536,1280]{1,0:T(8,128)(2,1)S(1)}, f32[1536,1280]{1,0:T(8,128)}) fusion(f32[1536,1280]{1,0:T(8,128)S(1)} %fusion.34, bf16[1536,768]{1,0:T(8,128)(2,1)S(1)} %multiply_convert_fusion.4, bf16[768,1280]{1,0:T(8,128)(2,1)S(1)} %bitcast.53), kind=kOutput, calls=%fused_computation.2 | convolution fusion | flops 3031695360 | bytes 23986176 | tf_op jit(solution)/shard_map/dot_general | solution.py:15
  151.5 3.5 convolution_convert_fusion.3
  155.4 4.4 %collective-permute-done.1 = bf16[1536,768]{1,0:T(8,128)(2,1)} collective-permute-done((bf16[1536,768]{1,0:T(8,128)(2,1)S(1)}, bf16[1536,768]{1,0:T(8,128)(2,1)}, u32[]{:S(2)}, u32[]{:S(2)}) %collective-permute-start.1) | collective-permute-done | bytes 2359328 | tf_op jit(solution)/shard_map/ppermute | solution.py:523
  159.8 4.1 %multiply_reduce_fusion.2 = (f32[1536]{0:T(1024)S(1)}, f32[1536,768]{1,0:T(8,128)S(1)}) fusion(bf16[1536,768]{1,0:T(8,128)(2,1)} %collective-permute-done.1, bf16[1536,768]{1,0:T(8,128)(2,1)S(1)} %convolution_convert_fusion.3, f32[768]{0:T(1024)S(1)} %convert_reduce_fusion.1, f32[1536,768]{1,0:T(8,128)} %copy-done, f32[1536]{0:T(1024)S(1)} %add_rsqrt_fusion.1), kind=kLoop, calls=%fused_computation.17 | loop fusion | flops 9435648 | bytes 14171136 | tf_op jit(solution)/shard_map/reduce_sum | solution.py:502
  165.6 2.5 fusion.3
  168.0 1.9 collective-permute-start.2
  170.0 9.9 %multiply_convert_fusion = (bf16[1536,1280]{1,0:T(8,128)(2,1)}, bf16[1536,1280]{1,0:T(8,128)(2,1)}) fusion(f32[1536,1280]{1,0:T(8,128)S(1)} %bitcast.61, f32[1536,1280]{1,0:T(8,128)} %get-tuple-element.100, bf16[768,1280]{1,0:T(8,128)(2,1)S(1)} %bitcast.58, f32[1536,768]{1,0:T(8,128)S(1)} %get-tuple-element.85), kind=kOutput, calls=%fused_computation | convolution fusion | flops 3046637568 | bytes 30277632 | tf_op jit(solution)/shard_map/dot_general | solution.py:15
  179.9 5.6 %fusion.35 = f32[1536,768]{1,0:T(8,128)S(1)} fusion(bf16[1536,1280]{1,0:T(8,128)(2,1)} %get-tuple-element.84, bf16[768,1280]{1,0:T(8,128)(2,1)S(1)} %bitcast.56), kind=kOutput, calls=%fused_computation.96 | convolution fusion | flops 3019898880 | bytes 10616832 | tf_op jit(solution)/shard_map/dot_general | solution.py:16
  185.6 3.5 add_convert_fusion
  189.8 4.6 %convolution_convert_fusion.2 = bf16[768,1280]{1,0:T(8,128)(2,1)} fusion(bf16[1536,768]{1,0:T(8,128)(2,1)S(1)} %copy-done.7, bf16[1536,1280]{1,0:T(8,128)(2,1)S(1)} %copy-done.30), kind=kOutput, calls=%fused_computation.24 | convolution fusion | flops 3020881920 | bytes 8257536 | tf_op jit(solution)/shard_map/dot_general | solution.py:565
  194.4 4.5 %convolution_convert_fusion.1 = bf16[768,1280]{1,0:T(8,128)(2,1)} fusion(bf16[1536,768]{1,0:T(8,128)(2,1)S(1)} %copy-done.7, bf16[1536,1280]{1,0:T(8,128)(2,1)S(1)} %copy-done.29), kind=kOutput, calls=%fused_computation.23 | convolution fusion | flops 3020881920 | bytes 8257536 | tf_op jit(solution)/shard_map/dot_general | solution.py:565
  198.9 4.6 %convolution_convert_fusion = bf16[768,1280]{1,0:T(8,128)(2,1)} fusion(bf16[1536,1280]{1,0:T(8,128)(2,1)S(1)} %copy-done.27, f32[1536,768]{1,0:T(8,128)S(1)} %get-tuple-element.85), kind=kOutput, calls=%fused_computation.22 | convolution fusion | flops 3022061568 | bytes 10616832 | tf_op jit(solution)/shard_map/dot_general | solution.py:565
  203.6 2.4 multiply_reduce_fusion
  206.9 6.8 %fusion.29 = (bf16[1536,768]{1,0:T(8,128)(2,1)S(1)}, f32[1536,768]{1,0:T(8,128)}) fusion(f32[1536]{0:T(1024)S(1)} %broadcast_multiply_fusion, f32[1536,768]{1,0:T(8,128)} %copy-done, f32[768]{0:T(1024)S(1)} %convert_reduce_fusion.1, f32[1536,768]{1,0:T(8,128)} %copy-done.1, bf16[1536,768]{1,0:T(8,128)(2,1)} %copy-done.3, ...), kind=kLoop, calls=%fused_computation.90 | loop fusion | flops 11796480 | bytes 21249024 | tf_op jit(solution)/shard_map/convert_element_type | solution.py:574
  213.7 2.5 convolution_convert_fusion.5.dm
  216.3 71.8 %attn_bwd_reduce.1 = (bf16[3,1536,512]{2,1,0:T(8,128)(2,1)}, bf16[4,48,640]{2,1,0:T(8,128)(2,1)}, bf16[4,48,640]{2,1,0:T(8,128)(2,1)}, bf16[4,48,640]{2,1,0:T(8,...) custom-call(bf16[4,1536,128]{2,1,0:T(8,128)(2,1)} %get-tuple-element.48.q_s, ...), custom_call_target="tpu_custom_call" | custom-call | tf_op jit(solution)/shard_map/attn_bwd_reduce/pallas_call | solution.py:398
  288.1 62.4 %token_grad_reduce.1 = (bf16[48,1280]{1,0:T(8,128)(2,1)}, bf16[48,1280]{1,0:T(8,128)(2,1)}, bf16[48,1280]{1,0:T(8,128)(2,1)}, bf16[48,1664]{1,0:T(8,128)(2,1)}, bf16[6,256,768]{2,1,0:T(8,128)(2,1)}) custom-call(bf16[3,1536,512]{2,1,0:T(8,128)(2,1)} %get-tuple-element.57.dqkv, bf16[768,1536]{1,0:T(8,128)(2,1)} %get-tuple-element.58.tok_t, ...), custom_call_target="tpu_custom_call" | custom-call | tf_op jit(solution)/shard_map/token_grad_reduce/pallas_call | solution.py:488
  350.5 4.2 %collective-permute-start.4 = (bf16[48,1664]{1,0:T(8,128)(2,1)}, bf16[48,1664]{1,0:T(8,128)(2,1)S(1)}, u32[]{:S(2)}, u32[]{:S(2)}) collective-permute-start(bf16[48,1664]{1,0:T(8,128)(2,1)} %get-tuple-element.67), channel_id=1, source_target_pairs={{0,0},{3,3},{1,2},{2,1},{4,4},{7,7},{5,6},{6,5},{8,8},{11,11},{9,1... | collective-permute-start | bytes 479240 | tf_op jit(solution)/shard_map/ppermute | solution.py:596
  354.7 4.2 %bitcast_convert_fusion = f32[1536,768]{1,0:T(8,128)} fusion(bf16[6,256,768]{2,1,0:T(8,128)(2,1)} %get-tuple-element.66), kind=kLoop, calls=%fused_computation.28 | loop fusion | flops 1179648 | bytes 7077888 | tf_op jit(solution)/shard_map/convert_element_type | solution.py:582
  359.0 3.4 broadcast_select_fusion
  362.4 1.9 collective-permute-start.5
  366.4 4.8 %collective-permute-done.5 = bf16[48,3840]{1,0:T(8,128)(2,1)S(1)} collective-permute-done((bf16[48,3840]{1,0:T(8,128)(2,1)S(1)}, bf16[48,3840]{1,0:T(8,128)(2,1)S(1)}, u32[]{:S(2)}, u32[]{:S(2)}) %collective-permute-start.5) | collective-permute-done | bytes 368672 | tf_op jit(solution)/shard_map/ppermute | solution.py:596
  (119 shorter events, 15.9 us)
Async XLA Ops:
  11.7 3.3 copy-start.8
  11.7 4.0 %copy-start.9 = (f32[48,1280]{1,0:T(8,128)S(1)}, f32[48,1280]{1,0:T(8,128)}, u32[]{:S(2)}) copy-start(f32[48,1280]{1,0:T(8,128)} %param.21) | copy-start | bytes 737284
  11.8 4.6 %copy-start.10 = (f32[1280,48]{0,1:T(8,128)S(1)}, f32[1280,48]{0,1:T(8,128)}, u32[]{:S(2)}) copy-start(f32[1280,48]{0,1:T(8,128)} %param.22) | copy-start | bytes 737284
  126.6 9.3 %copy-start.5 = (bf16[1536,768]{1,0:T(8,128)(2,1)S(1)}, bf16[1536,768]{1,0:T(8,128)(2,1)}, u32[]{:S(2)}) copy-start(bf16[1536,768]{1,0:T(8,128)(2,1)} %get-tuple-element.41) | copy-start | bytes 7077892
  131.0 4.9 %collective-permute-start = (bf16[1536,768]{1,0:T(8,128)(2,1)}, bf16[1536,768]{1,0:T(8,128)(2,1)}, u32[]{:S(2)}, u32[]{:S(2)}) collective-permute-start(bf16[1536,768]{1,0:T(8,128)(2,1)} %convolution_convert_fusion.4), channel_id=1, source_target_pairs={{0,2},{2,0},{1,3},{3,1},{4,6},{6,4},{5,7},{7,5},{8,10},{10,8},{9,1... | collective-permute-start | bytes 7077896 | tf_op jit(solution)/shard_map/ppermute | solution.py:523
  139.4 6.3 %copy-start = (f32[1536,768]{1,0:T(8,128)}, f32[1536,768]{1,0:T(8,128)S(1)}, u32[]{:S(2)}) copy-start(f32[1536,768]{1,0:T(8,128)S(1)} %get-tuple-element.82) | copy-start | bytes 14155780
  139.9 5.8 %copy-start.6 = (bf16[1536,768]{1,0:T(8,128)(2,1)}, bf16[1536,768]{1,0:T(8,128)(2,1)S(1)}, u32[]{:S(2)}) copy-start(bf16[1536,768]{1,0:T(8,128)(2,1)S(1)} %multiply_convert_fusion.4) | copy-start | bytes 7077892
  142.4 3.3 copy-start.20
  145.7 5.8 %copy-start.28 = (f32[1536,1280]{1,0:T(8,128)}, f32[1536,1280]{1,0:T(8,128)S(1)}, u32[]{:S(2)}) copy-start(f32[1536,1280]{1,0:T(8,128)S(1)} %fusion.34) | copy-start | bytes 23592964
  145.7 5.8 %copy-start.24 = (bf16[4,2,2,48,1280]{4,3,2,1,0:T(8,128)(2,1)S(1)}, bf16[4,2,2,48,1280]{4,3,2,1,0:T(8,128)(2,1)}, u32[]{:S(2)}) copy-start(bf16[4,2,2,48,1280]{4,3,2,1,0:T(8,128)(2,1)} %get-tuple-element.47) | copy-start | bytes 5898244
  151.5 3.5 copy-start.26
  155.1 4.7 %collective-permute-start.1 = (bf16[1536,768]{1,0:T(8,128)(2,1)S(1)}, bf16[1536,768]{1,0:T(8,128)(2,1)}, u32[]{:S(2)}, u32[]{:S(2)}) collective-permute-start(bf16[1536,768]{1,0:T(8,128)(2,1)S(1)} %convolution_convert_fusion.3), channel_id=1, source_target_pairs={{0,2},{2,0},{1,3},{3,1},{4,6},{6,4},{5,7},{7,5},{8,10},{10,8},{9,1... | collective-permute-start | bytes 7077896 | tf_op jit(solution)/shard_map/ppermute | solution.py:523
  155.4 8.5 %copy-start.4 = (bf16[1536,768]{1,0:T(8,128)(2,1)S(1)}, bf16[1536,768]{1,0:T(8,128)(2,1)}, u32[]{:S(2)}) copy-start(bf16[1536,768]{1,0:T(8,128)(2,1)} %get-tuple-element.52) | copy-start | bytes 7077892
  163.9 6.1 %slice-start.2 = ((s8[7864320]{0:T(1024)(128)(4,1)}), s8[4194304]{0:T(1024)(128)(4,1)S(1)}, s32[]{:S(2)}) async-start(s8[7864320]{0:T(1024)(128)(4,1)} %bitcast.60), calls=%async_computation.2 | async-start | bytes 8388608
  165.5 4.4 %copy-start.25 = (bf16[4,2,2,48,1280]{4,3,2,1,0:T(8,128)(2,1)S(1)}, bf16[4,2,2,48,1280]{4,3,2,1,0:T(8,128)(2,1)}, u32[]{:S(2)}) copy-start(bf16[4,2,2,48,1280]{4,3,2,1,0:T(8,128)(2,1)} %get-tuple-element.47) | copy-start | bytes 5898244
  165.5 4.4 %slice-start.3 = ((s8[7864320]{0:T(1024)(128)(4,1)}), s8[3670016]{0:T(1024)(128)(4,1)S(1)}, s32[]{:S(2)}) async-start(s8[7864320]{0:T(1024)(128)(4,1)} %bitcast.60), calls=%async_computation.3 | async-start | bytes 7340032
  168.0 35.5 %copy-start.1 = (f32[1536,768]{1,0:T(8,128)}, f32[1536,768]{1,0:T(8,128)S(1)}, u32[]{:S(2)}) copy-start(f32[1536,768]{1,0:T(8,128)S(1)} %get-tuple-element.85) | copy-start | bytes 14155780
  168.0 190.9 %collective-permute-start.2 = (bf16[1536,768]{1,0:T(8,128)(2,1)}, bf16[1536,768]{1,0:T(8,128)(2,1)}, u32[]{:S(2)}, u32[]{:S(2)}) collective-permute-start(bf16[1536,768]{1,0:T(8,128)(2,1)} %get-tuple-element.86), channel_id=1, source_target_pairs={{1,2},{2,1},{5,6},{6,5},{9,10},{10,9},{13,14},{14,13},{17,18},{18,... | collective-permute-start | bytes 7077896 | tf_op jit(solution)/shard_map/ppermute | solution.py:578
  170.0 9.9 %copy-start.23 = (bf16[4,2,2,48,1280]{4,3,2,1,0:T(8,128)(2,1)S(1)}, bf16[4,2,2,48,1280]{4,3,2,1,0:T(8,128)(2,1)}, u32[]{:S(2)}) copy-start(bf16[4,2,2,48,1280]{4,3,2,1,0:T(8,128)(2,1)} %get-tuple-element.45) | copy-start | bytes 5898244
  179.9 5.6 %copy-start.21 = (bf16[4,2,2,48,1280]{4,3,2,1,0:T(8,128)(2,1)S(1)}, bf16[4,2,2,48,1280]{4,3,2,1,0:T(8,128)(2,1)}, u32[]{:S(2)}) copy-start(bf16[4,2,2,48,1280]{4,3,2,1,0:T(8,128)(2,1)} %get-tuple-element.46) | copy-start | bytes 5898244
  179.9 5.6 %copy-start.29 = (bf16[1536,1280]{1,0:T(8,128)(2,1)S(1)}, bf16[1536,1280]{1,0:T(8,128)(2,1)}, u32[]{:S(2)}) copy-start(bf16[1536,1280]{1,0:T(8,128)(2,1)} %get-tuple-element.83) | copy-start | bytes 11796484
  185.5 4.2 %copy-start.7 = (bf16[1536,768]{1,0:T(8,128)(2,1)S(1)}, bf16[1536,768]{1,0:T(8,128)(2,1)}, u32[]{:S(2)}) copy-start(bf16[1536,768]{1,0:T(8,128)(2,1)} %copy-done.6) | copy-start | bytes 7077892
  185.6 4.2 %copy-start.30 = (bf16[1536,1280]{1,0:T(8,128)(2,1)S(1)}, bf16[1536,1280]{1,0:T(8,128)(2,1)}, u32[]{:S(2)}) copy-start(bf16[1536,1280]{1,0:T(8,128)(2,1)} %get-tuple-element.84) | copy-start | bytes 11796484
  189.1 14.5 %collective-permute-start.3 = (bf16[1536,768]{1,0:T(8,128)(2,1)S(1)}, bf16[1536,768]{1,0:T(8,128)(2,1)S(1)}, u32[]{:S(2)}, u32[]{:S(2)}) collective-permute-start(bf16[1536,768]{1,0:T(8,128)(2,1)S(1)} %add_convert_fusion), channel_id=1, source_target_pairs={{0,2},{2,0},{1,3},{3,1},{4,6},{6,4},{5,7},{7,5},{8,10},{10,8},{9,1... | collective-permute-start | bytes 7077896 | tf_op jit(solution)/shard_map/ppermute | solution.py:523
  189.8 13.8 %slice-start = ((s8[4718592]{0:T(1024)(128)(4,1)}), s8[4194304]{0:T(1024)(128)(4,1)S(1)}, s32[]{:S(2)}) async-start(s8[4718592]{0:T(1024)(128)(4,1)} %bitcast.47), calls=%async_computation | async-start | bytes 8388608
  194.4 4.5 %copy-start.27 = (bf16[1536,1280]{1,0:T(8,128)(2,1)S(1)}, bf16[1536,1280]{1,0:T(8,128)(2,1)}, u32[]{:S(2)}) copy-start(bf16[1536,1280]{1,0:T(8,128)(2,1)} %copy-done.26) | copy-start | bytes 11796484
  194.4 9.1 %slice-start.1 = ((s8[4718592]{0:T(1024)(128)(4,1)}), s8[524288]{0:T(1024)(128)(4,1)S(1)}, s32[]{:S(2)}) async-start(s8[4718592]{0:T(1024)(128)(4,1)} %bitcast.47), calls=%async_computation.1 | async-start | bytes 1048576
  350.5 13.8 %collective-permute-start.4 = (bf16[48,1664]{1,0:T(8,128)(2,1)}, bf16[48,1664]{1,0:T(8,128)(2,1)S(1)}, u32[]{:S(2)}, u32[]{:S(2)}) collective-permute-start(bf16[48,1664]{1,0:T(8,128)(2,1)} %get-tuple-element.67), channel_id=1, source_target_pairs={{0,0},{3,3},{1,2},{2,1},{4,4},{7,7},{5,6},{6,5},{8,8},{11,11},{9,1... | collective-permute-start | bytes 479240 | tf_op jit(solution)/shard_map/ppermute | solution.py:596
  359.0 3.4 copy-start.11
  359.0 3.4 copy-start.12
  359.0 3.4 copy-start.13
  362.4 8.8 %collective-permute-start.5 = (bf16[48,3840]{1,0:T(8,128)(2,1)S(1)}, bf16[48,3840]{1,0:T(8,128)(2,1)S(1)}, u32[]{:S(2)}, u32[]{:S(2)}) collective-permute-start(bf16[48,3840]{1,0:T(8,128)(2,1)S(1)} %pad_maximum_fusion), channel_id=1, source_target_pairs={{0,0},{3,3},{1,2},{2,1},{4,4},{7,7},{5,6},{6,5},{8,8},{11,11},{9,1... | collective-permute-start | bytes 1105928 | tf_op jit(solution)/shard_map/ppermute | solution.py:596
  (9 other events, 23.7 us)
where the time goes:
time: 376 us; the launch traced here: 373 us
  Pallas kernels  241 us (64%)
  matrix products  54.1 us (14%)
  other arithmetic  37.1 us (10%)
  local copies, waits for them, and re-layouts  15.4 us (4%)
  waiting for transfers between devices  12.8 us (3%)
  starting transfers between devices  8.96 us (2%)
    pallas_call x1, Pallas kernels, fused_fwd(): pl.pallas_call(functools.partial(fused_fwd_kernel, n, cols, ff), out_shap...  107 us
    pallas_call x1, Pallas kernels, fused_bwd(): pl.pallas_call(functools.partial(fused_bwd_kernel, n, heads), out_shape=[...  71.8 us
    pallas_call x1, Pallas kernels, tail(): pl.pallas_call(functools.partial(tail_kernel, n, cols), out_shape=[S((48,...  62.4 us
    dot_general x4, matrix products, dot(): return jnp.dot(a, b, preferred_element_type=f32)  21.5 us
    dot_general x5, matrix products, dot_nt(): return lax.dot_general(a, b, NT, preferred_element_type=f32)  18.8 us
    dot_general x3, matrix products, on_device(): lax.dot_general(a, b, (((0,), (0,)), ((), ())), preferred_element_type=f32)  13.7 us
    ppermute x3, waiting for transfers between devices, core_sum(): return part.astype(f32) + lax.ppermute(part, 'c', CORE).astype(f32)  7.92 us
    reduce_sum x2, other arithmetic, rms_forward(): inverse = lax.rsqrt(jnp.mean(resid * resid, -1, keepdims=True) + NORM_EPS)  7.58 us
  transfers between devices with their start and end apart: 6, of which 3 were waited for; matrix products, arithmetic and copies ran while one was open for 15% of the time, Pallas kernels for 36%

commit v1 on v0

--- a/solution.py
+++ b/solution.py
@@ -171,60 +171,59 @@
         pl.semaphore_signal(barrier,inc=1,device_id=w,device_id_type=MESH)
     pl.semaphore_wait(barrier,len(where))
 
-class Halve:
-    def __init__(self,source,one,two,send,recv,first):
-        self.source,self.one,self.two,self.first=source,one,two,first
+def remote(s,d,ss,rs,w):
+    return pltpu.make_async_remote_copy(src_ref=s,dst_ref=d,send_sem=ss,recv_sem=rs,device_id=w,device_id_type=MESH)
+
+class First:
+    def __init__(self,source,one,sem,first="y"):
+        self.source,self.one,self.first=source,one,first
         z,y,m=place()
         self.y,self.m=y,m
-        to=peers(z,y,m)
-        a,b=(0,1) if first=="y" else (1,0)
-        copy=lambda s,d,k,w: pltpu.make_async_remote_copy(src_ref=s,dst_ref=d,send_sem=send.at[k],recv_sem=recv.at[k],device_id=w,device_id_type=MESH)
-        self.c1=copy(source.at[:,1-y] if first=="y" else source.at[:,:,1-m],one,0,to[a])
-        self.c2=copy(one.at[:,(1-m) if first=="y" else (1-y)],two,1,to[b])
-    def start(self):
-        self.c1.start()
-    def second(self):
-        self.c1.wait_recv()
+        ny,nx=peers(z,y,m)[:2]
+        self.copy=remote(source.at[:,1-y],one,sem.at[0],sem.at[1],ny) if first=="y" else remote(source.at[:,:,1-m],one,sem.at[0],sem.at[1],nx)
+    def start(self): self.copy.start()
+    def finish(self):
+        self.copy.wait_recv()
         def add(i,_):
             zz=i//2; o=i-zz*2
             mine=self.source[zz,self.y,o] if self.first=="y" else self.source[zz,o,self.m]
             self.one[zz,o]=(self.one[zz,o].astype(f32)+mine.astype(f32)).astype(bf)
             return 0
         lax.fori_loop(0,8,add,0)
-        self.c2.start()
-    def third(self):
-        self.c2.wait_recv()
-        keep=self.m if self.first=="y" else self.y
+    def drain(self): self.copy.wait_send()
+
+class Second:
+    def __init__(self,one,two,sem,first="y"):
+        self.one,self.two=one,two
+        z,y,m=place()
+        ny,nx=peers(z,y,m)[:2]
+        self.keep=m if first=="y" else y
+        self.copy=remote(one.at[:,1-self.keep],two,sem.at[0],sem.at[1],nx if first=="y" else ny)
+    def start(self): self.copy.start()
+    def finish(self):
+        self.copy.wait_recv()
         def add(zz,_):
-            self.two[zz]=(self.two[zz].astype(f32)+self.one[zz,keep].astype(f32)).astype(bf)
+            self.two[zz]=(self.two[zz].astype(f32)+self.one[zz,self.keep].astype(f32)).astype(bf)
             return 0
         lax.fori_loop(0,4,add,0)
-    def drain(self):
-        self.c1.wait_send(); self.c2.wait_send()
-
-class Quarter:
+    def drain(self): self.copy.wait_send()
+
+class Third:
     def __init__(self,two,three,out,send,recv):
         self.two,self.three,self.out=two,three,out
         z,y,m=place()
         self.z=z
         to=peers(z,y,m)
-        self.c3=[pltpu.make_async_remote_copy(src_ref=two.at[lax.rem(z+s,4)],dst_ref=three.at[s-1],send_sem=send.at[s-1],recv_sem=recv.at[s-1],
-            device_id=to[1+s],device_id_type=MESH) for s in (1,2,3)]
+        self.copies=[remote(two.at[lax.rem(z+s,4)],three.at[s-1],send.at[s-1],recv.at[s-1],to[1+s]) for s in (1,2,3)]
     def start(self):
-        for c in self.c3: c.start()
+        for c in self.copies: c.start()
     def finish(self):
-        for c in self.c3: c.wait_recv()
+        for c in self.copies: c.wait_recv()
         t=self.two[self.z].astype(f32)
         for s in range(3): t=t+self.three[s].astype(f32)
         self.out[...]=t.astype(bf)
     def drain(self):
-        for c in self.c3: c.wait_send()
-
-def halve_scratch(c):
-    return [pltpu.VMEM((4,2,48,c),bf),pltpu.SemaphoreType.DMA((2,)),pltpu.SemaphoreType.DMA((2,))]
-def quarter_scratch(c):
-    return [pltpu.VMEM((3,48,c),bf),pltpu.SemaphoreType.DMA((3,)),pltpu.SemaphoreType.DMA((3,))]
-
+        for c in self.copies: c.wait_send()
 
 class Gather:
     def __init__(self,full,cols,send,recv,first):
@@ -253,8 +252,8 @@
 def both(c,m):
     return [{"c":1-c},{"c":1-c,"m":1-m}]
 
-def fused_fwd_kernel(n,cols,ff,tok_i,og_i,cos_i,sin_i,start_i,a_i,o_i,g_i,u_i,d_i,
-        tok,og,cos,sin,start,wa,wo,wg,wu,wd,q_o,k_o,v_o,m_t,mixed,lse,tok_t,wt,
+def fused_fwd_kernel(n,cols,ff,tok_i,cos_i,sin_i,start_i,a_i,o_i,g_i,u_i,d_i,
+        tok,cos,sin,start,wa,wo,wg,wu,wd,q_o,k_o,v_o,m_t,mixed,lse,tok_t,wt,
         wq_s,q_t,v_t,swap_s,swap_r,put_s,put_r,*sems):
     z,y,m=place(); c=lax.axis_index("c")
     own=c==m
@@ -265,7 +264,7 @@
     shards=[(a_i,wa),(g_i,wg),(u_i,wu),(d_i,wd),(o_i,wo)]
     put_far=[remote(s,d.at[z,y,c],put_s.at[i],put_r.at[i],diag) for i,(s,d) in enumerate(shards)]
     put_near=[pltpu.make_async_copy(s,d.at[z,y,c],put_r.at[i]) for i,(s,d) in enumerate(shards)]
-    packs=[(tok_i,tok),(cos_i,cos),(sin_i,sin),(start_i,start),(og_i,og)]
+    packs=[(tok_i,tok),(cos_i,cos),(sin_i,sin),(start_i,start)]
     swap_far=[remote(s,d,swap_s.at[i],swap_r.at[i],{"c":1-c}) for i,(s,d) in enumerate(packs)]
     swap_near=[pltpu.make_async_copy(s,d,swap_r.at[i]) for i,(s,d) in enumerate(packs)]
     @pl.when(own)
@@ -335,7 +334,7 @@
     def _():
         for x in put_far: x.wait_send()
 
-def fused_fwd(tok,og,cos,sin,start,a,o,g,u,d,cols):
+def fused_fwd(tok,cos,sin,start,a,o,g,u,d,cols):
     n,width=tok.shape; heads=cols//HD; pr=heads//2; ff=g.shape[1]
     V=pl.BlockSpec(memory_space=pltpu.VMEM); A=pl.BlockSpec(memory_space=pl.ANY)
     S=jax.ShapeDtypeStruct
@@ -343,99 +342,123 @@
     wide=lambda a: S((4,2,2)+a.shape,bf)
     dma=lambda k: pltpu.SemaphoreType.DMA((k,))
     return pl.pallas_call(functools.partial(fused_fwd_kernel,n,cols,ff),
-      out_shape=[like(tok),like(og),like(cos),like(sin),like(start),wide(a),wide(o),wide(g),wide(u),wide(d),
+      out_shape=[like(tok),like(cos),like(sin),like(start),wide(a),wide(o),wide(g),wide(u),wide(d),
         S((pr,n,128),bf),S((pr,n,128),bf),S((pr,n,128),bf),S((pr,128,n),f32),S((n,pr*128),bf),S((heads,n),f32),S((width,n),bf),S((3,pr*128,width),bf)],
-      in_specs=[A]*10,out_specs=[V]*18,
+      in_specs=[A]*9,out_specs=[V]*17,
       scratch_shapes=[pltpu.VMEM((5,pr*128,width),bf),pltpu.VMEM((pr,128,n),bf),pltpu.VMEM((pr,128,n),bf),
-        dma(5),dma(5),dma(5),dma(5)]+[dma(5)]*22,
-      compiler_params=pltpu.CompilerParams(vmem_limit_bytes=60<<20,collective_id=0,has_side_effects=True),name="attn_fwd_gather")(tok,og,cos,sin,start,a,o,g,u,d)
-
-def fused_bwd_kernel(n,heads,q_s,k_s,v_s,m_t,dm,lse,start,cos,sin,gg,gu,gd,dqkv,t0,t1,t2,t3,t4,t5,q_t,k_t,dm_t,dm_s,dq_t,dk_s,dv_s,dd,*scr):
-    z,y,m=place()
-    greet(peers(z,y,m))
+        dma(4),dma(4),dma(5),dma(5)]+[dma(5)]*22,
+      compiler_params=pltpu.CompilerParams(vmem_limit_bytes=60<<20,collective_id=0,has_side_effects=True),name="attn_fwd_gather")(tok,cos,sin,start,a,o,g,u,d)
+
+def fused_bwd_kernel(n,cols,q_s,k_s,v_s,dm,lse,start,cos,sin,d0,d1,m_i,g_i,u_i,o_i,tok_i,wt_i,d_one,od,og,ou,oo,oh0,oh1,gtok,
+        q_t,k_t,dm_t,dq_t,dk_s,dv_s,dd,dqkv,gg,gu,gow,tok_t,wt,d_buf,ga0,ga1,term,other,summed,load_s,d_sem,core_s,core_r,far_s,far_r,fin_s,fin_r,*scr):
+    z,y,m=place(); c=lax.axis_index("c")
+    own=c==m
+    diag={"c":1-c,"m":1-m}
+    loads=[pltpu.make_async_copy(a,b,load_s.at[i]) for i,(a,b) in enumerate(((m_i,dq_t),(g_i,gg),(u_i,gu),(o_i,gow),(tok_i,tok_t),(wt_i,wt)))]
+    for x in loads: x.start()
+    greet(peers(z,y,m)+both(c,m))
+    scr=list(scr)
+    def take(k):
+        got=scr[:k]
+        del scr[:k]
+        return got
     half=gg.shape[-1]//2
-    two=[t0,t1,t2,t3,t4,t5]
-    ch=[]
-    for k in range(6):
-        src=(gd,gg,gu)[k//2]
-        one,s,r=scr[3*k:3*k+3]
-        ch.append(Halve(src.at[:,:,:,:,(k%2)*half:(k%2)*half+half],one,two[k],s,r,"yx"[k%2]))
-    for x in ch: x.start()
-    P_=heads//2
+    srcs=[(g_i,gg,0,"y"),(g_i,gg,half,"x"),(u_i,gu,0,"y"),(u_i,gu,half,"y")]
+    firsts,seconds,thirds,lasts={},{},{},{}
+    for name,k in (("g0",0),("g1",1),("u0",2),("u1",3)):
+        _,own_ref,lo,first=srcs[k]
+        one,sem=take(2)
+        firsts[name]=First(own_ref.at[:,:,:,:,lo:lo+half],one,sem,first)
+        two,sem=take(2)
+        seconds[name]=Second(one,two,sem,first)
+    for name,src in (("o",gow),("h0",ga0),("h1",ga1)):
+        one,sem=take(2)
+        firsts[name]=First(src,one,sem)
+        two,sem=take(2)
+        seconds[name]=Second(one,two,sem)
+    for name,one in (("d0",d0),("d1",d1)):
+        two,sem=take(2)
+        seconds[name]=Second(one,two,sem)
+    fd,fg,fu,fo,fh0,fh1=take(6)
+    outs={"d0":fd.at[:,0:half],"d1":fd.at[:,half:2*half],"g0":fg.at[:,0:half],"g1":fg.at[:,half:2*half],"u0":fu.at[:,0:half],"u1":fu.at[:,half:2*half],
+        "o":fo,"h0":fh0,"h1":fh1}
+    for name,out in outs.items():
+        three,ss,rs=take(3)
+        thirds[name]=Third(seconds[name].two,three,out,ss,rs)
+    pairs={"d":(fd,od),"g":(fg,og),"u":(fu,ou),"o":(fo,oo),"h0":(fh0,oh0),"h1":(fh1,oh1)}
+    finals={k:remote(a,b,fin_s.at[i],fin_r.at[i],diag) for i,(k,(a,b)) in enumerate(pairs.items())}
+    def give(*names):
+        @pl.when(own)
+        def _():
+            for k in names: pairs[k][1][...]=pairs[k][0][...]
+        @pl.when(jnp.logical_not(own))
+        def _():
+            for k in names: finals[k].start()
+    def run(*steps):
+        for group,what,names in steps:
+            for k in names.split(): getattr(group[k],what)()
+    run((seconds,"start","d0 d1"))
+    loads[1].wait(); loads[2].wait()
+    run((firsts,"start","g0 u0 g1 u1"))
+    heads=cols//HD; P_=heads//2
     for p in range(P_):
         q_t[p]=q_s[p].T
         k_t[p]=k_s[p].T
-        dm_s[p]=dm[:,p*128:p*128+128]
-        dm_t[p]=dm_s[p].T
+        dm_t[p]=dm[p].T
+    loads[0].wait()
+    for p in range(P_):
         for half_ in range(2):
             r=slice(half_*64,half_*64+64)
-            dd[2*p+half_:2*p+half_+1,:]=jnp.sum(dm_t[p,r,:].astype(f32)*m_t[p,r,:],0,keepdims=True)
+            dd[2*p+half_:2*p+half_+1,:]=jnp.sum(dm_t[p,r,:].astype(f32)*dq_t[p,r,:],0,keepdims=True)
     dk_s[...]=jnp.zeros_like(dk_s); dv_s[...]=jnp.zeros_like(dv_s)
-    plan={1:[(0,"second"),(1,"second")],3:[(0,"third"),(1,"third")],4:[(2,"second"),(3,"second")],6:[(2,"third"),(3,"third")],7:[(4,"second"),(5,"second")]}
+    loads[3].wait(); loads[4].wait(); loads[5].wait()
+    sc=HD**-0.5
+    width=tok_t.shape[0]; quarter=width//4; hp=P_*128; part=hp//2
+    def raw_grads(half_):
+        for p in range(half_*P_//2,(half_+1)*P_//2):
+            dqkv[0,:,p*128:p*128+128]=rope_back(dq_t[p].T*sc,cos[...],sin[...]).astype(bf)
+            dqkv[1,:,p*128:p*128+128]=rope_back(dk_s[p]*sc,cos[...],sin[...]).astype(bf)
+            dqkv[2,:,p*128:p*128+128]=dv_s[p].astype(bf)
+    def weight_grads(half_):
+        ga=(ga0,ga1)[half_]
+        w=ga.shape[-1]; hc=cols//2
+        maps=[]
+        for j in range(3):
+            rr=lax.broadcasted_iota(jnp.int32,(part,w),0); cc=lax.broadcasted_iota(jnp.int32,(part,w),1)
+            hh=rr//64; dd_=rr-hh*64
+            maps.append(jnp.where((dd_<HD)&(cc==j*hc+hh*HD+dd_),1.0,0.0).astype(bf))
+        def body(i,_):
+            r=pl.ds(pl.multiple_of(i*quarter,quarter),quarter)
+            t=0.0
+            for j in range(3):
+                t=t+dot(dot(tok_t[r,:],dqkv[j,:,half_*part:(half_+1)*part]).astype(bf),maps[j])
+            ga[i]=t.astype(bf).reshape(2,2,quarter//4,w)
+            return 0
+        lax.fori_loop(0,4,body,0)
+    def middle():
+        raw_grads(0)
+        weight_grads(0)
+    events={1:[lambda: run((seconds,"finish","d0 d1"),(thirds,"start","d0 d1"),(firsts,"finish","g0"),(seconds,"start","g0"))],
+        3:[lambda: run((firsts,"finish","u0 g1"),(seconds,"start","u0 g1"),(firsts,"start","o")),middle,lambda: run((firsts,"start","h0"))],
+        4:[lambda: run((thirds,"finish","d0 d1")),lambda: give("d"),lambda: run((seconds,"finish","g0"),(thirds,"start","g0"))],
+        5:[lambda: run((firsts,"finish","u1"),(seconds,"start","u1"),(seconds,"finish","u0"),(thirds,"start","u0"))],
+        6:[lambda: run((seconds,"finish","g1"),(thirds,"start","g1"))]}
     def body(h,_):
         for i in range(n//QB):
-            bwd_head(h,i,q_t,q_s,k_s,k_t,v_s,dm_t,dm_s,lse,dd,start,dq_t,dk_s,dv_s)
-        for at,todo in plan.items():
+            bwd_head(h,i,q_t,q_s,k_s,k_t,v_s,dm_t,dm,lse,dd,start,dq_t,dk_s,dv_s)
+        for at,calls in events.items():
             @pl.when(h==at)
             def _():
-                for k,what in todo: getattr(ch[k],what)()
+                for call in calls: call()
         return 0
     lax.fori_loop(0,heads,body,0)
-    sc=HD**-0.5
-    for p in range(P_):
-        dqkv[0,:,p*128:p*128+128]=rope_back(dq_t[p].T*sc,cos[...],sin[...]).astype(bf)
-        dqkv[1,:,p*128:p*128+128]=rope_back(dk_s[p]*sc,cos[...],sin[...]).astype(bf)
-        dqkv[2,:,p*128:p*128+128]=dv_s[p].astype(bf)
-    ch[4].third(); ch[5].third()
-    for x in ch: x.drain()
-
-def fused_bwd(q_s,k_s,v_s,m_t,dm,lse,start,cos,sin,gg,gu,gd):
-    pr,n,_=q_s.shape; heads=2*pr
-    V=pl.BlockSpec(memory_space=pltpu.VMEM)
-    S=jax.ShapeDtypeStruct
-    ff=gg.shape[1]
-    cut=lambda a: a.reshape(4,2,2,48,ff)
-    return pl.pallas_call(functools.partial(fused_bwd_kernel,n,heads),
-      out_shape=[S((3,n,pr*128),bf)]+[S((4,48,ff//2),bf)]*6,
-      in_specs=[V]*12,out_specs=[V]*7,
-      scratch_shapes=[pltpu.VMEM((pr,128,n),bf),pltpu.VMEM((pr,128,n),bf),pltpu.VMEM((pr,128,n),bf),pltpu.VMEM((pr,n,128),bf),pltpu.VMEM((pr,128,n),f32),pltpu.VMEM((pr,n,128),f32),pltpu.VMEM((pr,n,128),f32),pltpu.VMEM((heads,n),f32)]
-        +sum([halve_scratch(ff//2) for _ in range(6)],[]),
-      compiler_params=pltpu.CompilerParams(vmem_limit_bytes=60<<20,collective_id=1,has_side_effects=True),name="attn_bwd_reduce")(
-        q_s,k_s,v_s,m_t,dm,lse,start,cos,sin,cut(gg),cut(gu),cut(gd))
-
-def tail_kernel(n,cols,dqkv,tok_t,wt,dattn,mixed,d_one,gains,t0,t1,t2,t3,t4,t5,og,ou,od,oa,gtok,ga,term,other,summed,core_s,core_r,far_s,far_r,
-        h0,h0s,h0r,h1,h1s,h1r,two0,two1,*scr):
-    z,y,m=place(); c=lax.axis_index("c")
-    own=c==m
-    greet(peers(z,y,m)+both(c,m))
-    half=t0.shape[-1]
-    ff=[]
-    for k,t in enumerate((t0,t1,t2,t3,t4,t5)):
-        three,s,r=scr[3*k:3*k+3]
-        ff.append(Quarter(t,three,(od,og,ou)[k//2].at[:,(k%2)*half:(k%2)*half+half],s,r))
-    for x in ff: x.start()
-    w=ga.shape[-1]; mid=2*cols+128
-    c0,c1=ga.at[:,:,:,:,0:mid],ga.at[:,:,:,:,mid:w]
-    halves=[Halve(c0,h0,two0,h0s,h0r,"y"),Halve(c1,h1,two1,h1s,h1r,"y")]
-    quarters=[Quarter(two0,scr[18],oa.at[:,0:mid],scr[19],scr[20]),Quarter(two1,scr[21],oa.at[:,mid:w],scr[22],scr[23])]
-    put=spread(cols//HD*64,cols,False)
-    width=tok_t.shape[0]; part=width//2
-    def pack(val): return val.reshape(2,2,2,48,val.shape[-1])
-    for i in range(2):
-        zz=slice(2*i,2*i+2); rows=slice(i*part,(i+1)*part)
-        ga[zz,:,:,:,0:128]=pack(gains[rows,:])
-        ga[zz,:,:,:,128:128+cols]=pack(dot_nt_t(dattn[:,rows].T,mixed[...],put))
-        ga[zz,:,:,:,128+cols:128+2*cols]=pack(dot_nt_t(tok_t[rows,:],dqkv[0],put))
-    halves[0].start()
-    for i in range(2):
-        zz=slice(2*i,2*i+2); rows=slice(i*part,(i+1)*part)
-        for j in (1,2):
-            ga[zz,:,:,:,128+(j+1)*cols:128+(j+2)*cols]=pack(dot_nt_t(tok_t[rows,:],dqkv[j],put))
-    halves[1].start()
+    raw_grads(1)
     nb=n//QB
-    def cross(b): return pltpu.make_async_remote_copy(src_ref=term.at[b],dst_ref=other.at[b],send_sem=core_s.at[b],recv_sem=core_r.at[b],device_id={"c":1-c},device_id_type=MESH)
-    def far(b): return pltpu.make_async_remote_copy(src_ref=summed.at[b],dst_ref=gtok.at[b],send_sem=far_s.at[b],recv_sem=far_r.at[b],device_id={"c":1-c,"m":1-m},device_id_type=MESH)
+    def cross(b): return remote(term.at[b],other.at[b],core_s.at[b],core_r.at[b],{"c":1-c})
+    def far(b): return remote(summed.at[b],gtok.at[b],far_s.at[b],far_r.at[b],diag)
     def near(b): return pltpu.make_async_copy(summed.at[b],gtok.at[b],far_r.at[b])
+    def fetch(b): return pltpu.make_async_copy(d_one.at[b],d_buf.at[lax.rem(b,2)],d_sem.at[lax.rem(b,2)])
+    fetch(0).start(); fetch(1).start()
     def make(b,_):
         rows=pl.ds(pl.multiple_of(b*QB,QB),QB)
         t=dot(dqkv[0,rows,:],wt[0])+dot(dqkv[1,rows,:],wt[1])+dot(dqkv[2,rows,:],wt[2])
@@ -443,10 +466,14 @@
         cross(b).start()
         return 0
     lax.fori_loop(0,nb,make,0)
+    run((seconds,"finish","u1"),(thirds,"start","u1"),(firsts,"finish","o"),(seconds,"start","o"))
     def total(b,_):
-        rows=pl.ds(pl.multiple_of(b*QB,QB),QB)
         cross(b).wait_recv()
-        summed[b]=(d_one[rows,:]+(term[b].astype(f32)+other[b].astype(f32))).astype(bf)
+        fetch(b).wait()
+        summed[b]=(d_buf[lax.rem(b,2)]+(term[b].astype(f32)+other[b].astype(f32))).astype(bf)
+        @pl.when(b+2<nb)
+        def _():
+            fetch(b+2).start()
         @pl.when(own)
         def _():
             near(b).start()
@@ -454,15 +481,23 @@
         def _():
             far(b).start()
         return 0
-    lax.fori_loop(0,nb,total,0)
-    halves[0].second()
-    for x in ff[:2]: x.finish()
-    halves[1].second()
-    for x in ff[2:]: x.finish()
-    halves[0].third(); quarters[0].start()
-    halves[1].third(); quarters[1].start()
-    quarters[0].finish(); quarters[1].finish()
-    for x in ff+halves+quarters: x.drain()
+    lax.fori_loop(0,1,total,0)
+    weight_grads(1)
+    run((firsts,"start","h1"))
+    lax.fori_loop(1,2,total,0)
+    run((firsts,"finish","h0"),(seconds,"start","h0"),(seconds,"finish","o"),(thirds,"start","o"))
+    lax.fori_loop(2,4,total,0)
+    run((thirds,"finish","g0 g1 u0 u1"))
+    run((firsts,"finish","h1"),(seconds,"start","h1"))
+    lax.fori_loop(4,nb,total,0)
+    run((seconds,"finish","h0"),(thirds,"start","h0"),(thirds,"finish","o"))
+    give("g","u","o")
+    run((seconds,"finish","h1"),(thirds,"start","h1"),(thirds,"finish","h0"))
+    give("h0")
+    run((thirds,"finish","h1"))
+    give("h1")
+    for group in (firsts,seconds,thirds):
+        for x in group.values(): x.drain()
     def drain(b,_):
         cross(b).wait_send()
         @pl.when(own)
@@ -474,29 +509,200 @@
             far(b).wait_send()
         return 0
     lax.fori_loop(0,nb,drain,0)
+    @pl.when(jnp.logical_not(own))
+    def _():
+        for x in finals.values():
+            x.wait_recv()
+            x.wait_send()
+
+def fused_bwd(q_s,k_s,v_s,m_t,dm,lse,start,cos,sin,gg,gu,gow,d0,d1,tok_t,wt,d_one,cols):
+    pr,n,_=q_s.shape; heads=2*pr; width=tok_t.shape[0]; nb=n//QB
+    V=pl.BlockSpec(memory_space=pltpu.VMEM); A=pl.BlockSpec(memory_space=pl.ANY)
+    S=jax.ShapeDtypeStruct
+    ff=gg.shape[-1]; r=gg.shape[-2]; w=gow.shape[-1]; h=ff//2; hw=-(-3*cols//2//128)*128
+    vm=pltpu.VMEM
+    dma=lambda k: pltpu.SemaphoreType.DMA((k,))
+    blocks=(nb,QB,width)
+    like=lambda a: vm(a.shape,a.dtype)
+    one=lambda k: [vm((4,2,r,k),bf),dma(2)]
+    two=lambda k: [vm((4,r,k),bf),dma(2)]
+    three=lambda k: [vm((3,r,k),bf),dma(3),dma(3)]
+    return pl.pallas_call(functools.partial(fused_bwd_kernel,n,cols),
+      out_shape=[S((r,ff),bf)]*3+[S((r,w),bf)]+[S((r,hw),bf)]*2+[S(blocks,bf)],
+      in_specs=[V]*10+[A]*7,out_specs=[V]*6+[A],
+      scratch_shapes=[vm((pr,128,n),bf)]*3+[vm((pr,128,n),f32),vm((pr,n,128),f32),vm((pr,n,128),f32),vm((heads,n),f32),vm((3,n,pr*128),bf),
+        like(gg),like(gu),like(gow),like(tok_t),like(wt),vm((2,QB,width),f32),vm((4,2,2,r,hw),bf),vm((4,2,2,r,hw),bf)]+[vm(blocks,bf)]*3
+        +[dma(6),dma(2)]+[dma(nb)]*4+[dma(6),dma(6)]
+        +(one(h)+two(h))*4+one(w)+two(w)+(one(hw)+two(hw))*2+two(h)*2
+        +[vm((r,ff),bf)]*3+[vm((r,w),bf)]+[vm((r,hw),bf)]*2+three(h)*6+three(w)+three(hw)*2,
+      compiler_params=pltpu.CompilerParams(vmem_limit_bytes=64<<20,collective_id=1,has_side_effects=True),name="attn_bwd_reduce")(
+        q_s,k_s,v_s,dm,lse,start,cos,sin,d0,d1,m_t,gg,gu,gow,tok_t,wt,d_one.reshape(blocks))
 
 def dot_nt_t(a,b,put):
     return dot(dot(a,b).astype(bf),put).astype(bf)
-
-def tail(dqkv,tok_t,wt,dattn,mixed,d_one,gains,twos,cols):
-    n,width=dattn.shape; ff=2*twos[0].shape[-1]; w=4*cols+128; mid=2*cols+128
-    V=pl.BlockSpec(memory_space=pltpu.VMEM); A=pl.BlockSpec(memory_space=pl.ANY)
-    S=jax.ShapeDtypeStruct
-    blocks=(n//QB,QB,width)
-    dma=lambda k: pltpu.SemaphoreType.DMA((k,))
-    half=lambda k: [pltpu.VMEM((4,2,48,k),bf),dma(2),dma(2)]
-    return pl.pallas_call(functools.partial(tail_kernel,n,cols),
-      out_shape=[S((48,ff),bf)]*3+[S((48,w),bf),S(blocks,bf)],
-      in_specs=[V]*13,out_specs=[V]*4+[A],
-      scratch_shapes=[pltpu.VMEM((4,2,2,48,w),bf),pltpu.VMEM(blocks,bf),pltpu.VMEM(blocks,bf),pltpu.VMEM(blocks,bf)]+[dma(n//QB)]*4
-        +halve_scratch(mid)+halve_scratch(w-mid)+[pltpu.VMEM((4,48,mid),bf),pltpu.VMEM((4,48,w-mid),bf)]
-        +sum([quarter_scratch(ff//2) for _ in range(6)],[])+quarter_scratch(mid)+quarter_scratch(w-mid),
-      compiler_params=pltpu.CompilerParams(vmem_limit_bytes=60<<20,collective_id=2,has_side_effects=True),name="token_grad_reduce")(
-        dqkv,tok_t,wt,dattn,mixed,d_one,gains,*twos)
 
 NORM_EPS=1e-05
 DIAG=[(0,0),(3,3),(1,2),(2,1)]
 CORE=[(0,1),(1,0)]
+
+def cross_copies(n,part,other,send,recv,c):
+    def one(b): return pltpu.make_async_remote_copy(src_ref=part.at[b],dst_ref=other.at[b],send_sem=send.at[b],recv_sem=recv.at[b],device_id={"c":1-c},device_id_type=MESH)
+    return one
+
+def norm_of(r):
+    inv=lax.rsqrt(jnp.mean(r*r,-1,keepdims=True)+NORM_EPS)
+    return r*inv,inv
+
+def norm_back(e,nrm,inv):
+    return inv*(e-nrm*jnp.mean(e*nrm,-1,keepdims=True))
+
+def ffn_kernel(n,cols,tok,og,mixed,ofull,wg,wu,wd,ga,gb,output,gg,gu,d_one,dm,gow,one0,one1,
+        out_t,t1,t2,act,normed,inv1,hb_t,dff_t,part,oa,of,oh,summed,gsum,gd,og_s,og_r,a_s,a_r,f_s,f_r,h_s,h_r,x_s,x_r,s0,s1):
+    z,y,m=place(); c=lax.axis_index("c")
+    own=c==m
+    greet(peers(z,y,m)+both(c,m))
+    nb=n//QB
+    grad_far=pltpu.make_async_remote_copy(src_ref=og,dst_ref=summed,send_sem=og_s,recv_sem=og_r,device_id={"c":1-c},device_id_type=MESH)
+    grad_near=pltpu.make_async_copy(og,summed,og_r)
+    def rows_of(b): return pl.ds(pl.multiple_of(b*QB,QB),QB)
+    ca,cf,ch=[cross_copies(n,part,o,ss,rs,c) for o,ss,rs in ((oa,a_s,a_r),(of,f_s,f_r),(oh,h_s,h_r))]
+    def far(b): return pltpu.make_async_remote_copy(src_ref=summed.at[b],dst_ref=output.at[b],send_sem=x_s.at[b],recv_sem=x_r.at[b],device_id={"c":1-c,"m":1-m},device_id_type=MESH)
+    def near(b): return pltpu.make_async_copy(summed.at[b],output.at[b],x_r.at[b])
+    out_t[...]=dot_nt(ofull[...],spread(cols//HD*64,cols,False)).astype(bf)
+    def attn_part(b,_):
+        part[b]=dot_nt(mixed[rows_of(b),:],out_t[...]).astype(bf)
+        ca(b).start()
+        return 0
+    lax.fori_loop(0,nb,attn_part,0)
+    @pl.when(own)
+    def _():
+        grad_far.start()
+        grad_near.start()
+    def forward(b,_):
+        rows=rows_of(b)
+        ca(b).wait_recv()
+        r=tok[rows,:].astype(f32)+(part[b].astype(f32)+oa[b].astype(f32))
+        nrm,inv=norm_of(r)
+        normed[rows,:]=nrm
+        inv1[rows,:]=inv
+        hb=(nrm*ga[...]).astype(bf)
+        hb_t[:,rows]=hb.T
+        gate=dot(hb,wg[...]); up=dot(hb,wu[...])
+        sg=jax.nn.sigmoid(gate)
+        gs=gate*sg
+        a=(gs*up).astype(bf)
+        act[rows,:]=a
+        t2[rows,:]=gs.astype(bf)
+        t1[rows,:]=(up*sg*(1.0+gate*(1.0-sg))).astype(bf)
+        ca(b).wait_send()
+        part[b]=dot_nt(a,wd[...]).astype(bf)
+        cf(b).start()
+        return 0
+    lax.fori_loop(0,nb,forward,0)
+    @pl.when(own)
+    def _():
+        grad_near.wait()
+        grad_far.wait_send()
+    @pl.when(jnp.logical_not(own))
+    def _():
+        grad_far.wait_recv()
+    gsum[...]=jnp.zeros_like(gsum)
+    def fold(v): return jnp.sum(v.reshape(QB//8,8,v.shape[-1]),0)
+    def norm_two(b,_):
+        rows=rows_of(b)
+        cf(b).wait_recv()
+        nrm,inv=norm_of(normed[rows,:]*ga[...]+(part[b].astype(f32)+of[b].astype(f32)))
+        g=summed[b].astype(f32)
+        summed[b]=(nrm*gb[...]).astype(bf)
+        @pl.when(own)
+        def _():
+            near(b).start()
+        @pl.when(jnp.logical_not(own))
+        def _():
+            far(b).start()
+        gsum[8:16,:]+=fold(g*nrm)
+        d2=norm_back(g*gb[...],nrm,inv)
+        d_one[rows,:]=d2
+        df=d2.astype(bf)
+        oa[b]=df
+        dff_t[:,rows]=df.T
+        return 0
+    lax.fori_loop(0,nb,norm_two,0)
+    width=hb_t.shape[0]; quarter=width//4; ff=act.shape[1]
+    def rows4(i): return pl.ds(pl.multiple_of(i*quarter,quarter),quarter)
+    def down_grad(i,_):
+        gd[i]=dot(dff_t[rows4(i),:],act[...]).astype(bf).reshape(2,2,quarter//4,ff)
+        return 0
+    lax.fori_loop(0,4,down_grad,0)
+    h2=ff//2
+    ch2=[First(gd.at[:,:,:,:,0:h2],one0,s0),First(gd.at[:,:,:,:,h2:ff],one1,s1)]
+    for x in ch2: x.start()
+    def backward(b,_):
+        rows=rows_of(b)
+        da=dot(oa[b],wd[...])
+        dg=(da*t1[rows,:].astype(f32)).astype(bf); du=(da*t2[rows,:].astype(f32)).astype(bf)
+        t1[rows,:]=dg; t2[rows,:]=du
+        cf(b).wait_send()
+        part[b]=(dot_nt(dg,wg[...])+dot_nt(du,wu[...])).astype(bf)
+        ch(b).start()
+        return 0
+    lax.fori_loop(0,nb,backward,0)
+    def grads(i,_):
+        gg[i]=dot(hb_t[rows4(i),:],t1[...]).astype(bf).reshape(2,2,quarter//4,ff)
+        gu[i]=dot(hb_t[rows4(i),:],t2[...]).astype(bf).reshape(2,2,quarter//4,ff)
+        return 0
+    lax.fori_loop(0,4,grads,0)
+    def last(b,_):
+        rows=rows_of(b)
+        ch(b).wait_recv()
+        dh=d_one[rows,:]+(part[b].astype(f32)+oh[b].astype(f32))
+        nrm=normed[rows,:]
+        gsum[0:8,:]+=fold(dh*nrm)
+        d1=norm_back(dh*ga[...],nrm,inv1[rows,:])
+        d_one[rows,:]=d1
+        da=d1.astype(bf)
+        hb_t[:,rows]=da.T
+        back=dot(da,out_t[...]).astype(bf)
+        for p in range(dm.shape[0]): dm[p,rows,:]=back[:,p*128:p*128+128]
+        return 0
+    lax.fori_loop(0,nb,last,0)
+    put=spread(cols//HD*64,cols,False)
+    def out_grads(i,_):
+        gow[i,:,:,:,128:128+cols]=dot_nt_t(hb_t[rows4(i),:],mixed[...],put).reshape(2,2,quarter//4,cols)
+        return 0
+    lax.fori_loop(0,4,out_grads,0)
+    line=lax.broadcasted_iota(jnp.int32,(128,width),0)
+    both_gains=jnp.where(line==0,jnp.sum(gsum[0:8,:],0,keepdims=True),jnp.where(line==1,jnp.sum(gsum[8:16,:],0,keepdims=True),0.0))
+    gow[:,:,:,:,0:128]=both_gains.T.astype(bf).reshape(4,2,2,quarter//4,128)
+    for x in ch2: x.finish()
+    for x in ch2: x.drain()
+    def drain(b,_):
+        ch(b).wait_send()
+        @pl.when(own)
+        def _():
+            near(b).wait()
+        @pl.when(jnp.logical_not(own))
+        def _():
+            far(b).wait_recv()
+            far(b).wait_send()
+        return 0
+    lax.fori_loop(0,nb,drain,0)
+
+def ffn_call(tok,og,mixed,ofull,wg,wu,wd,ga,gb,cols):
+    n,width=tok.shape; ff=wg.shape[1]; hp=mixed.shape[1]; nb=n//QB
+    V=pl.BlockSpec(memory_space=pltpu.VMEM); A=pl.BlockSpec(memory_space=pl.ANY)
+    S=jax.ShapeDtypeStruct
+    blocks=(nb,QB,width); r=width//16
+    dma=pltpu.SemaphoreType.DMA((nb,))
+    vm=pltpu.VMEM
+    return pl.pallas_call(functools.partial(ffn_kernel,n,cols),
+      out_shape=[S(blocks,bf)]+[S((4,2,2,r,ff),bf)]*2+[S((n,width),f32),S((hp//128,n,128),bf),S((4,2,2,r,cols+128),bf)]+[S((4,2,r,ff//2),bf)]*2,
+      in_specs=[V,A]+[V]*7,out_specs=[A]+[V]*7,
+      scratch_shapes=[vm((width,hp),bf),vm((n,ff),bf),vm((n,ff),bf),vm((n,ff),bf),vm((n,width),f32),vm((n,1),f32),vm((width,n),bf),vm((width,n),bf),
+        vm(blocks,bf),vm(blocks,bf),vm(blocks,bf),vm(blocks,bf),vm(blocks,bf),vm((16,width),f32),vm((4,2,2,r,ff),bf),
+        pltpu.SemaphoreType.DMA,pltpu.SemaphoreType.DMA]+[dma]*8+[pltpu.SemaphoreType.DMA((2,))]*2,
+      compiler_params=pltpu.CompilerParams(vmem_limit_bytes=64<<20,collective_id=3,has_side_effects=True),name="ffn")(
+        tok,og.reshape(blocks),mixed,ofull,wg,wu,wd,ga[None],gb[None])
 
 def rms_forward(resid):
     inverse=lax.rsqrt(jnp.mean(resid*resid,-1,keepdims=True)+NORM_EPS)
@@ -513,11 +719,10 @@
     return start
 
 def rope_tables(positions):
-    half=HD//2
-    fr=jnp.exp(jnp.arange(half,dtype=f32)*(-2.0*math.log(10000.0)/HD))
+    lane=jnp.arange(128,dtype=jnp.int32)%64
+    fr=jnp.where(lane<HD,jnp.exp((lane%(HD//2)).astype(f32)*(-2.0*math.log(10000.0)/HD)),0.0)
     a=positions.astype(f32)[:,None]*fr[None,:]
-    c,s=jnp.cos(a),jnp.sin(a); z=jnp.zeros((positions.shape[0],64-HD),f32)
-    return jnp.concatenate([c,c,z,c,c,z],1),jnp.concatenate([s,s,z,s,s,z],1)
+    return jnp.cos(a),jnp.sin(a)
 
 def core_sum(part):
     return part.astype(f32)+lax.ppermute(part,"c",CORE).astype(f32)
@@ -538,8 +743,8 @@
     def gather(a):
         return lax.all_gather(lax.ppermute(a,("c","m"),DIAG),("q","m"),axis=0,tiled=True)
     if quad:
-        tokens,out_grad,cos,sin,start,afull,ofull,gate_w,up_w,down_t,q,k,v,m_t,mixed,lse,tok_t,wt=fused_fwd(
-            tokens,out_grad,cos,sin,start,apack,cast(w_out).T,cast(w_gate),cast(w_up),cast(w_down).T,cols)
+        tokens,cos,sin,start,afull,ofull,gate_w,up_w,down_t,q,k,v,m_t,mixed,lse,tok_t,wt=fused_fwd(
+            tokens,cos,sin,start,apack,cast(w_out).T,cast(w_gate),cast(w_up),cast(w_down).T,cols)
         afull,ofull,gate_w,up_w,down_t=[a.reshape(width,a.shape[-1]) for a in (afull,ofull,gate_w,up_w,down_t)]
     else:
         afull,ofull,gate_w,up_w,down_t=[gather(a) for a in (apack,cast(w_out).T,cast(w_gate),cast(w_up),cast(w_down).T)]
@@ -548,39 +753,43 @@
     put=spread(hp,cols,False)
     out_t=dot_nt(ofull,put).astype(bf)
     gain_a=afull[:,3*cols].astype(f32); gain_b=afull[:,3*cols+1].astype(f32)
-    attn=core_sum(dot_nt(mixed,out_t).astype(bf))
-    normed_one,inv_one=rms_forward(tokens.astype(f32)+attn)
-    hidden=normed_one*gain_a
-    hb=hidden.astype(bf)
-    gate=dot(hb,gate_w); up=dot(hb,up_w)
-    sg=jax.nn.sigmoid(gate)
-    act=(gate*sg*up).astype(bf)
-    ffn=core_sum(dot_nt(act,down_t).astype(bf))
-    normed_two,inv_two=rms_forward(hidden+ffn)
-    output=(normed_two*gain_b).astype(bf)
-    g=out_grad.astype(f32)
-    g_gain_two=jnp.sum(g*normed_two,0)
-    d_two=rms_backward(g*gain_b,normed_two,inv_two)
-    d_ffn=d_two.astype(bf)
-    tn=lambda a,b: lax.dot_general(a,b,(((0,),(0,)),((),())),preferred_element_type=f32)
-    d_act=dot(d_ffn,down_t)
-    d_up=(d_act*gate*sg).astype(bf)
-    d_gate=(d_act*up*sg*(1.0+gate*(1.0-sg))).astype(bf)
-    hterm=(dot_nt(d_gate,gate_w)+dot_nt(d_up,up_w)).astype(bf)
-    gff=[tn(hb,d_gate).astype(bf),tn(hb,d_up).astype(bf),tn(d_ffn,act).astype(bf)]
-    d_hidden=d_two+core_sum(hterm)
-    g_gain_one=jnp.sum(d_hidden*normed_one,0)
-    d_one=rms_backward(d_hidden*gain_a,normed_one,inv_one)
-    d_attn=d_one.astype(bf)
-    dm=dot(d_attn,out_t).astype(bf)
-    ggain=jnp.pad(jnp.stack([g_gain_one,g_gain_two],1),((0,0),(0,126))).astype(bf)
     own=lax.axis_index("c")==lax.axis_index("m")
-    output=jnp.where(own,output,lax.ppermute(output,("c","m"),[(1,2),(2,1)]))
     if quad:
-        dqkv,*twos=fused_bwd(q,k,v,m_t,dm,lse,start,cos,sin,*gff)
-        *sff,sat,gtok=tail(dqkv,tok_t,wt,d_attn,mixed,d_one,ggain,twos,cols)
-        gtok=gtok.reshape(n,width).astype(f32)
+        output,gg,gu,d_one,dm,gow,*downs=ffn_call(tokens,out_grad,mixed,ofull,gate_w,up_w,down_t,gain_a,gain_b,cols)
+        output=output.reshape(n,width)
+        sdown,sgate,sup,sout,sh0,sh1,gtok=[a.astype(f32) for a in fused_bwd(q,k,v,m_t,dm,lse,start,cos,sin,gg,gu,gow,*downs,tok_t,wt,d_one,cols)]
+        hc=cols//2
+        sq,sk,sv=[jnp.concatenate([a[:,j*hc:(j+1)*hc] for a in (sh0,sh1)],1) for j in range(3)]
+        return (output,gtok.reshape(n,width),sq,sk,sv,sout[:,128:].T,sout[:,0],sgate,sup,sdown.T,sout[:,1])
     else:
+        attn=core_sum(dot_nt(mixed,out_t).astype(bf))
+        normed_one,inv_one=rms_forward(tokens.astype(f32)+attn)
+        hidden=normed_one*gain_a
+        hb=hidden.astype(bf)
+        gate=dot(hb,gate_w); up=dot(hb,up_w)
+        sg=jax.nn.sigmoid(gate)
+        act=(gate*sg*up).astype(bf)
+        ffn=core_sum(dot_nt(act,down_t).astype(bf))
+        normed_two,inv_two=rms_forward(hidden+ffn)
+        output=(normed_two*gain_b).astype(bf)
+        g=out_grad.astype(f32)
+        g_gain_two=jnp.sum(g*normed_two,0)
+        d_two=rms_backward(g*gain_b,normed_two,inv_two)
+        d_ffn=d_two.astype(bf)
+        tn=lambda a,b: lax.dot_general(a,b,(((0,),(0,)),((),())),preferred_element_type=f32)
+        d_act=dot(d_ffn,down_t)
+        d_up=(d_act*gate*sg).astype(bf)
+        d_gate=(d_act*up*sg*(1.0+gate*(1.0-sg))).astype(bf)
+        hterm=(dot_nt(d_gate,gate_w)+dot_nt(d_up,up_w)).astype(bf)
+        gff=[tn(hb,d_gate).astype(bf),tn(hb,d_up).astype(bf),tn(d_ffn,act).astype(bf)]
+        d_hidden=d_two+core_sum(hterm)
+        g_gain_one=jnp.sum(d_hidden*normed_one,0)
+        d_one=rms_backward(d_hidden*gain_a,normed_one,inv_one)
+        d_attn=d_one.astype(bf)
+        dm=dot(d_attn,out_t).astype(bf)
+        output=jnp.where(own,output,lax.ppermute(output,("c","m"),[(1,2),(2,1)]))
+
+        ggain=jnp.pad(jnp.stack([g_gain_one,g_gain_two],1),((0,0),(0,126))).astype(bf)
         dqkv=attn_bwd(q,k,v,m_t,dm,lse,start,cos,sin)
         term=0.0; gqkv=[]
         for j in range(3):
@@ -593,9 +802,9 @@
         gatt=jnp.concatenate([ggain,g_out]+gqkv,1)
         add=lambda a: lax.psum_scatter(a,("q","m"),scatter_dimension=0,tiled=True)
         sff,sat=[add(a) for a in gff],add(gatt)
-    sff,sat=lax.ppermute(jnp.concatenate(sff,1),("c","m"),DIAG).astype(f32),lax.ppermute(sat,("c","m"),DIAG).astype(f32)
-    piece=lambda j: sat[:,128+j*cols:128+(j+1)*cols]
-    return (output,gtok,piece(1),piece(2),piece(3),piece(0).T,sat[:,0],sff[:,:ff],sff[:,ff:2*ff],sff[:,2*ff:].T,sat[:,1])
+        sff,sat=lax.ppermute(jnp.concatenate(sff,1),("c","m"),DIAG).astype(f32),lax.ppermute(sat,("c","m"),DIAG).astype(f32)
+        piece=lambda j: sat[:,128+j*cols:128+(j+1)*cols]
+        return (output,gtok,piece(1),piece(2),piece(3),piece(0).T,sat[:,0],sff[:,:ff],sff[:,ff:2*ff],sff[:,2*ff:].T,sat[:,1])
 
 def solution(mesh):
     dp,mp=mesh.shape["dp"],mesh.shape["mp"]

time: 376 us -> 319 us (0.85)
  matrix products: 54.1 us -> 0 us
  Pallas kernels: 241 us -> 280 us
  waiting for transfers between devices: 12.8 us -> 0 us
  starting transfers between devices: 8.96 us -> 0 us
  other arithmetic: 37.1 us -> 28.4 us
  local copies, waits for them, and re-layouts: 15.4 us -> 7.36 us
    dot_general x12 -> x0, matrix products: 54.1 us -> none  [the longest x4 21.5 us: dot(): return jnp.dot(a, b, preferred_element_type=f32)]
    pallas_call x2, Pallas kernels: 134 us -> 174 us  [the longest x1 107 us: fused_bwd(): pl.pallas_call(functools.partial(fused_bwd_kernel, n, cols), out_shape=[S...]
    ppermute x6 -> x0, waiting for transfers between devices: 12.8 us -> none  [the longest x3 7.92 us: core_sum(): return part.astype(f32) + lax.ppermute(part, 'c', CORE).astype(f32)]
    reduce_sum x4 -> x0, other arithmetic: 11.6 us -> none  [the longest x2 7.58 us: rms_forward(): inverse = lax.rsqrt(jnp.mean(resid * resid, -1, keepdims=True) + NORM_EPS)]
    ppermute x6 -> x0, starting transfers between devices: 8.96 us -> none  [the longest x1 4.22 us: on_device(): lax.ppermute(sat, ('c', 'm'), DIAG).astype(f32)]
    convert_element_type x5 -> x3, other arithmetic: 11.5 us -> 4.18 us  [on_device(): a.astype(f32)]
    concatenate x2 -> x0, local copies, waits for them, and re-layouts: 5.41 us -> none  [the longest x1 2.97 us: rope_tables(): jnp.concatenate([c, c, z, c, c, z], 1)]
    convert_element_type x5, other arithmetic: 1.35 us -> 5.88 us  [on_device(): cast = lambda a: a.astype(bf)]
  transfers between devices with their start and end apart: 6 -> 0, of which waited for: 3 -> 0; matrix products, arithmetic and copies ran while one was open for 15% -> 0% of each run, Pallas kernels for 36% -> 0%
where the time goes in v1:
time: 319 us
  Pallas kernels  280 us (88%)
  other arithmetic  28.4 us (9%)
  local copies, waits for them, and re-layouts  7.36 us (2%)
    pallas_call x1, Pallas kernels, fused_bwd(): pl.pallas_call(functools.partial(fused_bwd_kernel, n, cols), out_shape=[S...  107 us
    pallas_call x1, Pallas kernels, fused_fwd(): pl.pallas_call(functools.partial(fused_fwd_kernel, n, cols, ff), out_shap...  106 us
    pallas_call x1, Pallas kernels, ffn_call(): pl.pallas_call(functools.partial(ffn_kernel, n, cols), out_shape=[S(block...  67.2 us

profile of v1, /device:TPU:1, one launch (start us, length us, event | category | flops | bytes accessed | tf_op | source)
XLA Modules:
  0.0 318.6 jit_solution(11424205838186804316)
XLA Ops:
  0.7 0.7 convert_bitcast_fusion.3
  1.3 1.4 fusion.8
  4.6 1.3 compare_select_fusion.2.start_i
  5.9 0.7 subtract_convert_fusion
  6.7 0.9 convert_element_type.88
  7.6 0.9 convert_element_type.89
  8.5 0.9 convert_element_type.90
  9.3 0.7 fusion.1.a_i
  10.0 1.5 convert_bitcast_fusion.2.o_i
  11.5 1.6 convert_element_type.94.g_i
  13.1 1.6 convert_element_type.95.u_i
  14.7 1.6 convert_bitcast_fusion.1.d_i
  16.3 4.3 %multiply_sine_fusion = (f32[1536,128]{1,0:T(8,128)}, f32[1536,128]{1,0:T(8,128)}) fusion(f32[128]{0:T(128)S(1)} %compare_select_fusion.3, f32[1536]{0:T(1024)S(1)} %subtract_convert_fusion), kind=kLoop, calls=%fused_computation.1 | loop fusion | flops 196608 | bytes 1579520 | tf_op jit(solution)/shard_map/sin | solution.py:725
  20.6 106.3 %attn_fwd_gather.1 = (bf16[1536,768]{1,0:T(8,128)(2,1)}, f32[1536,128]{1,0:T(8,128)}, f32[1536,128]{1,0:T(8,128)}, s32[1,1536]{1,0:T(1,128)}, bf16[4,2,2,48,1280...) custom-call(bf16[1536,768]{1,0:T(8,128)(2,1)} %tok_i.1, ...), custom_call_target="tpu_custom_call" | custom-call | tf_op jit(solution)/shard_map/attn_fwd_gather/pallas_call | solution.py:344
  126.9 1.1 fusion.5
  128.2 0.6 bitcast_convert_fusion.1.gb
  128.9 0.6 bitcast_convert_fusion.2.ga
  129.5 67.2 %ffn.1 = (bf16[6,256,768]{2,1,0:T(8,128)(2,1)}, bf16[4,2,2,48,1280]{4,3,2,1,0:T(8,128)(2,1)}, bf16[4,2,2,48,1280]{4,3,2,1,0:T(8,128)(2,1)}, f32[1536,768]{1,0:T(...) custom-call(bf16[1536,768]{1,0:T(8,128)(2,1)} %get-tuple-element.43., ...), custom_call_target="tpu_custom_call" | custom-call | tf_op jit(solution)/shard_map/ffn/pallas_call | solution.py:698
  196.7 106.7 %attn_bwd_reduce.1 = (bf16[48,1280]{1,0:T(8,128)(2,1)}, bf16[48,1280]{1,0:T(8,128)(2,1)}, bf16[48,1280]{1,0:T(8,128)(2,1)}, bf16[48,512]{1,0:T(8,128)(2,1)}, bf1...) custom-call(bf16[4,1536,128]{2,1,0:T(8,128)(2,1)} %get-tuple-element.51.q_s, ...), custom_call_target="tpu_custom_call" | custom-call | tf_op jit(solution)/shard_map/attn_bwd_reduce/pallas_call | solution.py:530
  303.5 1.0 convert_element_type.103
  304.4 0.7 slice_reduce_fusion
  305.1 0.6 slice_bitcast_fusion
  305.8 0.9 fusion.6
  306.6 0.9 fusion.7
  307.5 0.7 pad_maximum_fusion.2
  308.2 0.7 pad_maximum_fusion.1
  309.0 0.7 pad_maximum_fusion
  309.7 1.6 convert_element_type.104
  311.3 1.6 convert_element_type.105
  312.9 1.6 convert_bitcast_fusion
  314.5 2.7 bitcast_convert_fusion
  317.2 1.4 copy.35
  (9 shorter events, 0.4 us)
Async XLA Ops:
  303.4 11.1 %copy-start = (bf16[6,256,768]{2,1,0:T(8,128)(2,1)S(1)}, bf16[6,256,768]{2,1,0:T(8,128)(2,1)}, u32[]{:S(2)}) copy-start(bf16[6,256,768]{2,1,0:T(8,128)(2,1)} %get-tuple-element.68) | copy-start | bytes 7077892
  314.5 2.7 copy-start.1

commit v2 on v1

--- a/solution.py
+++ b/solution.py
@@ -1,6 +1,8 @@
 import functools
 import math
-import jax, jax.numpy as jnp
+import jax
+import jax.numpy as jnp
+import numpy as np
 from jax import lax
 from jax.experimental import pallas as pl
 from jax.experimental.pallas import tpu as pltpu
@@ -23,29 +25,30 @@
     lo=(d<24)&(c==h*HD+d+24); hi=(d>=24)&(d<HD)&(c==h*HD+d-24)
     return jnp.where(lo,-1.0,jnp.where(hi,1.0,0.0)).astype(bf)
 
-def proj(tok,w,cos,sin,wq_s,q_s,k_s,v_s,n,cols):
+def proj_weights(w,wq_s,cols):
     hp=cols//HD*64
-    pairs=hp//128
     for m,(col,rot) in enumerate(((0,False),(0,True),(1,False),(1,True),(2,False))):
         if len(w.shape)==2:
             part=w[:,col*cols:(col+1)*cols]
         else:
             part=w[:,:,:,:,col*cols:(col+1)*cols].reshape(-1,cols)
         wq_s[m]=dot_nt(spread(hp,cols,rot),part).astype(bf)
+
+def proj(tok,cos,sin,wq_s,q_s,k_s,v_s,lo,hi):
     def body(b,_):
         rows=pl.ds(pl.multiple_of(b*QB,QB),QB)
         x=tok[rows,:]
         cs=cos[rows,:]; sn=sin[rows,:]
         for dst,a in ((q_s,0),(k_s,2)):
             raw=dot_nt(x,wq_s[a]); rt=dot_nt(x,wq_s[a+1])
-            for p in range(pairs):
+            for p in range(dst.shape[0]):
                 l=slice(p*128,p*128+128)
                 dst[p,rows,:]=(raw[:,l]*cs+rt[:,l]*sn).astype(bf)
         raw=dot_nt(x,wq_s[4])
-        for p in range(pairs):
+        for p in range(v_s.shape[0]):
             v_s[p,rows,:]=raw[:,p*128:p*128+128].astype(bf)
         return 0
-    lax.fori_loop(0,n//QB,body,0)
+    lax.fori_loop(lo,hi,body,0)
 
 def masks(kk0,nk,i,start):
     kidx=lax.broadcasted_iota(jnp.int32,(nk,QB),0)+kk0
@@ -72,7 +75,8 @@
     lse[pl.ds(h,1),qq]=m*C2+jnp.log2(l)
 
 def fwd_kernel(n,cols,tok,w,cos,sin,start,q_o,k_o,v_o,m_t,mixed,lse,wq_s,q_t,v_t):
-    proj(tok,w,cos,sin,wq_s,q_o,k_o,v_o,n,cols)
+    proj_weights(w,wq_s,cols)
+    proj(tok,cos,sin,wq_s,q_o,k_o,v_o,0,n//QB)
     heads=cols//HD
     for p in range(heads//2):
         q_t[p]=q_o[p].T
@@ -208,6 +212,36 @@
         lax.fori_loop(0,4,add,0)
     def drain(self): self.copy.wait_send()
 
+class SecondZ:
+    def __init__(self,one,two,three,send,recv):
+        self.one,self.two,self.three=one,two,three
+        z,y,m=place()
+        self.z=z
+        to=peers(z,y,m)
+        self.copies=[remote(one.at[lax.rem(z+s,4)],three.at[s-1],send.at[s-1],recv.at[s-1],to[1+s]) for s in (1,2,3)]
+    def start(self):
+        for c in self.copies: c.start()
+    def finish(self):
+        for c in self.copies: c.wait_recv()
+        for o in range(2):
+            t=self.one[self.z,o].astype(f32)
+            for s in range(3): t=t+self.three[s,o].astype(f32)
+            self.two[o]=t.astype(bf)
+    def drain(self):
+        for c in self.copies: c.wait_send()
+
+class ThirdX:
+    def __init__(self,two,other,out,sem):
+        self.two,self.other,self.out=two,other,out
+        z,y,m=place()
+        self.m=m
+        self.copy=remote(two.at[1-m],other,sem.at[0],sem.at[1],{"m":1-m})
+    def start(self): self.copy.start()
+    def finish(self):
+        self.copy.wait_recv()
+        self.out[...]=(self.two[self.m].astype(f32)+self.other[...].astype(f32)).astype(bf)
+    def drain(self): self.copy.wait_send()
+
 class Third:
     def __init__(self,two,three,out,send,recv):
         self.two,self.three,self.out=two,three,out
@@ -226,97 +260,169 @@
         for c in self.copies: c.wait_send()
 
 class Gather:
-    def __init__(self,full,cols,send,recv,first):
-        z,y,m=place()
+    def __init__(self,shard,full,cols,stage,sem,sem_z,first):
+        z,y,m=place(); c=lax.axis_index("c")
         to=peers(z,y,m)
-        a,b=(0,1) if first=="y" else (1,0)
-        def copy(at,k,w):
-            return pltpu.make_async_remote_copy(src_ref=at,dst_ref=at,send_sem=send.at[k],recv_sem=recv.at[k],device_id=w,device_id_type=MESH)
-        self.along=[copy(full.at[z,y,m,:,cols],s-1,to[1+s]) for s in (1,2,3)]
-        self.c2=copy(full.at[:,y,m,:,cols],3,to[a])
-        self.c3=copy(full.at[:,:,m,:,cols] if first=="y" else full.at[:,y,:,:,cols],4,to[b])
+        src=shard.at[:,cols]
+        self.first=first
+        self.own=c==m
+        self.here=pltpu.make_async_copy(src,stage.at[z,y],sem.at[0])
+        self.along=[remote(src,stage.at[z,y],sem_z.at[0,s-1],sem_z.at[1,s-1],to[1+s]) for s in (1,2,3)]
+        a,b=(stage.at[:,y],full.at[:,y,c,:,cols]) if first=="x" else (stage,full.at[:,:,c,:,cols])
+        self.near_self=pltpu.make_async_copy(a,b,sem.at[1])
+        self.near=remote(a,b,sem.at[2],sem.at[3],{"c":1-c})
+        self.far_same=remote(a,b,sem.at[4],sem.at[5],{"m":1-m})
+        self.far_diag=remote(a,b,sem.at[4],sem.at[6],{"c":1-c,"m":1-m})
+        d=full.at[:,y,:,:,cols] if first=="x" else stage.at[:,y]
+        self.across=remote(d,d,sem.at[7],sem.at[8],to[0])
     def start(self):
+        self.here.start()
         for c in self.along: c.start()
+    def cross(self):
+        @pl.when(self.own)
+        def _():
+            self.near_self.start()
+            self.far_same.start()
+        @pl.when(jnp.logical_not(self.own))
+        def _():
+            self.far_diag.start()
+            self.near.start()
+    def crossed(self):
+        @pl.when(self.own)
+        def _():
+            self.near_self.wait()
+            self.near.wait_recv()
+        @pl.when(jnp.logical_not(self.own))
+        def _():
+            self.far_same.wait_recv()
+            self.far_diag.wait_recv()
     def second(self):
+        self.here.wait()
         for c in self.along: c.wait_recv()
-        self.c2.start()
+        if self.first=="x": self.cross()
+        else: self.across.start()
     def third(self):
-        self.c2.wait_recv()
-        self.c3.start()
+        if self.first=="x":
+            self.crossed()
+            self.across.start()
+        else:
+            self.across.wait_recv()
+            self.cross()
     def finish(self):
-        self.c3.wait_recv()
+        if self.first=="x": self.across.wait_recv()
+        else: self.crossed()
     def drain(self):
         for c in self.along: c.wait_send()
-        self.c2.wait_send(); self.c3.wait_send()
+        self.across.wait_send()
+        @pl.when(self.own)
+        def _():
+            self.far_same.wait_send()
+        @pl.when(jnp.logical_not(self.own))
+        def _():
+            self.far_diag.wait_send()
+            self.near.wait_send()
 
 def both(c,m):
     return [{"c":1-c},{"c":1-c,"m":1-m}]
 
-def fused_fwd_kernel(n,cols,ff,tok_i,cos_i,sin_i,start_i,a_i,o_i,g_i,u_i,d_i,
-        tok,cos,sin,start,wa,wo,wg,wu,wd,q_o,k_o,v_o,m_t,mixed,lse,tok_t,wt,
-        wq_s,q_t,v_t,swap_s,swap_r,put_s,put_r,*sems):
+def fused_fwd_kernel(n,cols,lengths,freq,tok_i,wq_i,wk_i,wv_i,wo_i,wg_i,wu_i,wd_i,g1_i,g2_i,
+        tok_o,cos_o,sin_o,q_o,k_o,v_o,tok_t_o,wt_o,start,ga,gb,wo,wg,wu,wd,m_t,mixed,lse,
+        tok,cos,sin,q_s,k_s,v_s,tok_t,wa,wq_s,q_t,v_t,docs_i,docs,a_b,o_b,g_b,u_b,d_b,swap_s,swap_r,out_s,*scr):
     z,y,m=place(); c=lax.axis_index("c")
     own=c==m
+    r=a_b.shape[0]; ff=g_b.shape[1]
+    eye=(lax.broadcasted_iota(jnp.int32,(r,r),0)==lax.broadcasted_iota(jnp.int32,(r,r),1)).astype(bf)
+    line=lax.broadcasted_iota(jnp.int32,(128,r),0)
+    gains=jnp.where(line==0,g1_i[...],jnp.where(line==1,g2_i[...],0.0)).astype(bf)
+    for j,w in enumerate((wq_i,wk_i,wv_i)): a_b[:,j*cols:(j+1)*cols]=w[...].astype(bf)
+    a_b[:,3*cols:]=dot_nt(eye,gains).astype(bf)
+    g_b[...]=wg_i[...].astype(bf)
+    u_b[...]=wu_i[...].astype(bf)
+    o_b[...]=wo_i[...].astype(bf)
+    d_b[...]=wd_i[...].astype(bf)
+    row=lax.broadcasted_iota(jnp.int32,(8,128),0)
+    table=jnp.zeros((8,128),jnp.int32)
+    for i in range(lengths.shape[1]): table=jnp.where(row==i,lengths[0,i],table)
+    docs_i[...]=table
     greet(peers(z,y,m)+both(c,m))
-    def remote(s,d,ss,rs,w):
-        return pltpu.make_async_remote_copy(src_ref=s,dst_ref=d,send_sem=ss,recv_sem=rs,device_id=w,device_id_type=MESH)
-    diag={"c":1-c,"m":1-m}
-    shards=[(a_i,wa),(g_i,wg),(u_i,wu),(d_i,wd),(o_i,wo)]
-    put_far=[remote(s,d.at[z,y,c],put_s.at[i],put_r.at[i],diag) for i,(s,d) in enumerate(shards)]
-    put_near=[pltpu.make_async_copy(s,d.at[z,y,c],put_r.at[i]) for i,(s,d) in enumerate(shards)]
-    packs=[(tok_i,tok),(cos_i,cos),(sin_i,sin),(start_i,start)]
-    swap_far=[remote(s,d,swap_s.at[i],swap_r.at[i],{"c":1-c}) for i,(s,d) in enumerate(packs)]
-    swap_near=[pltpu.make_async_copy(s,d,swap_r.at[i]) for i,(s,d) in enumerate(packs)]
-    @pl.when(own)
-    def _():
-        for x in put_near: x.start()
-        for a,b in zip(swap_near,swap_far):
-            a.start(); b.start()
-        put_near[0].wait()
-    @pl.when(jnp.logical_not(own))
-    def _():
-        for x in put_far: x.start()
-        put_far[0].wait_recv()
-    def ga(full,lo,hi,k,first): return Gather(full,slice(lo,hi),sems[2*k],sems[2*k+1],first)
-    ac=wa.shape[-1]; cut=[0,ac//1280*256,ac//2,ac//2+ac//1280*384,ac]
-    a=[ga(wa,cut[i],cut[i+1],i,"xy"[i%2]) for i in range(4)]
+    packs=[(docs_i,docs),(tok_i,tok)]
+    swap_far=[remote(a,b,swap_s.at[i],swap_r.at[i],{"c":1-c}) for i,(a,b) in enumerate(packs)]
+    swap_near=[pltpu.make_async_copy(a,b,swap_r.at[i]) for i,(a,b) in enumerate(packs)]
+    scr=list(scr)
+    def chunk(shard,full,lo,hi,first):
+        stage,sem,sem_z=scr[:3]
+        del scr[:3]
+        return Gather(shard,full,slice(lo,hi),stage,sem,sem_z,first)
+    cut=cuts(a_b.shape[1])
+    a=[chunk(a_b,wa,cut[i],cut[i+1],"xy"[i%2]) for i in range(4)]
     h2=ff//2
-    f=[ga(w,j*h2,j*h2+h2,4+2*i+j,"xy"[j]) for i,w in enumerate((wg,wu,wd)) for j in range(2)]
-    f.append(ga(wo,0,wo.shape[-1],10,"x"))
+    f=[chunk(b,w,j*h2,j*h2+h2,"xy"[j]) for b,w in ((g_b,wg),(u_b,wu),(d_b,wd)) for j in range(2)]
+    f.append(chunk(o_b,wo,0,cols,"x"))
     for x in a: x.start()
     @pl.when(own)
     def _():
-        for x in put_near[1:]: x.wait()
+        for x,w in zip(swap_near,swap_far):
+            x.start(); w.start()
+        swap_near[0].wait()
     @pl.when(jnp.logical_not(own))
     def _():
-        for x in put_far[1:]: x.wait_recv()
+        swap_far[0].wait_recv()
+    for x in f: x.start()
+    def begin(at):
+        end=jnp.zeros((1,1),jnp.int32); first=jnp.zeros(at.shape,jnp.int32)
+        for i in range(lengths.shape[1]-1):
+            end=end+docs[i:i+1,0:1]
+            first=jnp.where(at>=end,end,first)
+        return first
+    start[...]=begin(lax.broadcasted_iota(jnp.int32,(1,n),1))
+    def tables(b,_):
+        rows=pl.ds(pl.multiple_of(b*QB,QB),QB)
+        at=lax.broadcasted_iota(jnp.int32,(QB,128),0)+b*QB
+        angle=(at-begin(at)).astype(f32)*freq[...]
+        cos[rows,:]=jnp.cos(angle)
+        sin[rows,:]=jnp.sin(angle)
+        return 0
+    nb=n//QB
+    lax.fori_loop(0,nb//2,tables,0)
     a[0].second(); a[1].second()
-    for x in f: x.start()
+    lax.fori_loop(nb//2,nb,tables,0)
+    a[0].third(); a[1].third()
+    a[2].second(); a[3].second()
+    keep=[pltpu.make_async_copy(v,h,out_s.at[i]) for i,(v,h) in enumerate(((cos,cos_o),(sin,sin_o),(tok,tok_o),(tok_t,tok_t_o),(wq_s.at[0],wt_o.at[0]),(wq_s.at[2],wt_o.at[1]),
+        (wq_s.at[4],wt_o.at[2]),(q_s,q_o),(k_s,k_o),(v_s,v_o)))]
+    keep[0].start(); keep[1].start()
     @pl.when(own)
     def _():
-        for x in swap_near: x.wait()
+        swap_near[1].wait()
     @pl.when(jnp.logical_not(own))
     def _():
-        for x in swap_far: x.wait_recv()
-    a[0].third(); a[1].third()
-    a[2].second(); a[3].second()
-    tok_t[:tok_t.shape[0]//2,:]=tok[:,:tok_t.shape[0]//2].T
+        swap_far[1].wait_recv()
+    keep[2].start()
+    half=tok_t.shape[0]//2
+    tok_t[:half,:]=tok[:,:half].T
     a[2].third(); a[3].third()
-    tok_t[tok_t.shape[0]//2:,:]=tok[:,tok_t.shape[0]//2:].T
+    tok_t[half:,:]=tok[:,half:].T
+    keep[3].start()
     for x in a: x.finish()
     f[0].second(); f[1].second()
-    proj(tok,wa,cos,sin,wq_s,q_o,k_o,v_o,n,cols)
+    proj_weights(wa,wq_s,cols)
+    for x in keep[4:7]: x.start()
+    proj(tok,cos,sin,wq_s,q_s,k_s,v_s,0,nb//2)
     f[0].third(); f[1].third()
     f[2].second(); f[3].second()
-    for j in range(3): wt[j]=wq_s[2*j]
+    proj(tok,cos,sin,wq_s,q_s,k_s,v_s,nb//2,nb)
+    for x in keep[7:]: x.start()
+    rows=wa[:,:,:,:,3*cols:].reshape(-1,128).astype(f32).T
+    ga[...]=rows[0:1,:]
+    gb[...]=rows[1:2,:]
     heads=cols//HD
     for p in range(heads//2):
-        q_t[p]=q_o[p].T
-        v_t[p]=v_o[p].T
-    plan={1:[(4,"second"),(5,"second")],2:[(2,"third"),(3,"third")],3:[(6,"second")],4:[(4,"third"),(5,"third")],5:[(6,"third")]}
+        q_t[p]=q_s[p].T
+        v_t[p]=v_s[p].T
+    plan={0:[(2,"third"),(3,"third"),(4,"second"),(5,"second")],3:[(4,"third"),(5,"third"),(6,"second")],5:[(6,"third")]}
     def body(h,_):
-        for i in range(n//QB):
-            fwd_head(h,i,q_t,k_o,v_t,start,m_t,lse)
+        for i in range(nb):
+            fwd_head(h,i,q_t,k_s,v_t,start,m_t,lse)
         for at,todo in plan.items():
             @pl.when(h==at)
             def _():
@@ -327,30 +433,39 @@
         mixed[:,p*128:p*128+128]=m_t[p].T.astype(bf)
     for x in f: x.finish()
     for x in a+f: x.drain()
+    for x in keep: x.wait()
     @pl.when(own)
     def _():
         for x in swap_far: x.wait_send()
-    @pl.when(jnp.logical_not(own))
-    def _():
-        for x in put_far: x.wait_send()
-
-def fused_fwd(tok,cos,sin,start,a,o,g,u,d,cols):
-    n,width=tok.shape; heads=cols//HD; pr=heads//2; ff=g.shape[1]
-    V=pl.BlockSpec(memory_space=pltpu.VMEM); A=pl.BlockSpec(memory_space=pl.ANY)
+
+def cuts(width):
+    return [0,width//1280*384,width//2,width//2+width//1280*256,width]
+
+def fused_fwd(lengths,tok,wq,wk,wv,w_out,wg,wu,wd,g1,g2):
+    n,width=tok.shape; r,cols=wq.shape; heads=cols//HD; pr=heads//2; ff=wg.shape[1]; ac=3*cols+128
+    V=pl.BlockSpec(memory_space=pltpu.VMEM); A=pl.BlockSpec(memory_space=pl.ANY); M=pl.BlockSpec(memory_space=pltpu.SMEM)
     S=jax.ShapeDtypeStruct
-    like=lambda a: S(a.shape,a.dtype)
-    wide=lambda a: S((4,2,2)+a.shape,bf)
-    dma=lambda k: pltpu.SemaphoreType.DMA((k,))
-    return pl.pallas_call(functools.partial(fused_fwd_kernel,n,cols,ff),
-      out_shape=[like(tok),like(cos),like(sin),like(start),wide(a),wide(o),wide(g),wide(u),wide(d),
-        S((pr,n,128),bf),S((pr,n,128),bf),S((pr,n,128),bf),S((pr,128,n),f32),S((n,pr*128),bf),S((heads,n),f32),S((width,n),bf),S((3,pr*128,width),bf)],
-      in_specs=[A]*9,out_specs=[V]*17,
-      scratch_shapes=[pltpu.VMEM((5,pr*128,width),bf),pltpu.VMEM((pr,128,n),bf),pltpu.VMEM((pr,128,n),bf),
-        dma(4),dma(4),dma(5),dma(5)]+[dma(5)]*22,
-      compiler_params=pltpu.CompilerParams(vmem_limit_bytes=60<<20,collective_id=0,has_side_effects=True),name="attn_fwd_gather")(tok,cos,sin,start,a,o,g,u,d)
-
-def fused_bwd_kernel(n,cols,q_s,k_s,v_s,dm,lse,start,cos,sin,d0,d1,m_i,g_i,u_i,o_i,tok_i,wt_i,d_one,od,og,ou,oo,oh0,oh1,gtok,
-        q_t,k_t,dm_t,dq_t,dk_s,dv_s,dd,dqkv,gg,gu,gow,tok_t,wt,d_buf,ga0,ga1,term,other,summed,load_s,d_sem,core_s,core_r,far_s,far_r,fin_s,fin_r,*scr):
+    vm=pltpu.VMEM
+    dma=lambda *k: pltpu.SemaphoreType.DMA(k)
+    wide=lambda k: S((4,2,2,r,k),bf)
+    lane=np.arange(128)%64
+    freq=np.where(lane<HD,np.exp((lane%(HD//2)).astype(np.float32)*np.float32(-2.0*math.log(10000.0)/HD)),0.0).astype(np.float32)[None]
+    cut=cuts(ac)
+    sizes=[cut[i+1]-cut[i] for i in range(4)]+[ff//2]*6+[cols]
+    pair=(pr,n,128)
+    return pl.pallas_call(functools.partial(fused_fwd_kernel,n,cols),
+      out_shape=[S((n,width),bf),S((n,128),f32),S((n,128),f32),S(pair,bf),S(pair,bf),S(pair,bf),S((width,n),bf),S((3,pr*128,width),bf),
+        S((1,n),jnp.int32),S((1,width),f32),S((1,width),f32),wide(cols),wide(ff),wide(ff),wide(ff),S((pr,128,n),f32),S((n,pr*128),bf),S((heads,n),f32)],
+      in_specs=[M,V,A]+[V]*9,out_specs=[A]*8+[V]*10,
+      scratch_shapes=[vm((n,width),bf),vm((n,128),f32),vm((n,128),f32),vm(pair,bf),vm(pair,bf),vm(pair,bf),vm((width,n),bf),vm((4,2,2,r,ac),bf),
+        vm((5,pr*128,width),bf),vm((pr,128,n),bf),vm((pr,128,n),bf),vm((8,128),jnp.int32),vm((8,128),jnp.int32),
+        vm((r,ac),bf),vm((r,cols),bf),vm((r,ff),bf),vm((r,ff),bf),vm((r,ff),bf),dma(2),dma(2),dma(10)]
+        +sum([[vm((4,2,r,k),bf),dma(9),dma(2,3)] for k in sizes],[]),
+      compiler_params=pltpu.CompilerParams(vmem_limit_bytes=60<<20,collective_id=0,has_side_effects=True),name="attn_fwd_gather")(
+        lengths,jnp.asarray(freq),tok,wq,wk,wv,w_out,wg,wu,wd,g1[None],g2[None])
+
+def fused_bwd_kernel(n,cols,q_s,k_s,v_s,dm,lse,start,cos,sin,d0,d1,m_i,g_i,u_i,o_i,tok_i,wt_i,d_one,grads,gtok,
+        q_t,k_t,dm_t,dq_t,dk_s,dv_s,dd,dqkv,gg,gu,gow,tok_t,wt,d_buf,ga0,ga1,term,other,load_s,d_sem,core_s,core_r,far_s,far_r,fin_s,fin_r,*scr):
     z,y,m=place(); c=lax.axis_index("c")
     own=c==m
     diag={"c":1-c,"m":1-m}
@@ -363,29 +478,29 @@
         del scr[:k]
         return got
     half=gg.shape[-1]//2
-    srcs=[(g_i,gg,0,"y"),(g_i,gg,half,"x"),(u_i,gu,0,"y"),(u_i,gu,half,"y")]
-    firsts,seconds,thirds,lasts={},{},{},{}
-    for name,k in (("g0",0),("g1",1),("u0",2),("u1",3)):
-        _,own_ref,lo,first=srcs[k]
-        one,sem=take(2)
-        firsts[name]=First(own_ref.at[:,:,:,:,lo:lo+half],one,sem,first)
-        two,sem=take(2)
-        seconds[name]=Second(one,two,sem,first)
-    for name,src in (("o",gow),("h0",ga0),("h1",ga1)):
-        one,sem=take(2)
-        firsts[name]=First(src,one,sem)
-        two,sem=take(2)
-        seconds[name]=Second(one,two,sem)
-    for name,one in (("d0",d0),("d1",d1)):
-        two,sem=take(2)
-        seconds[name]=Second(one,two,sem)
-    fd,fg,fu,fo,fh0,fh1=take(6)
-    outs={"d0":fd.at[:,0:half],"d1":fd.at[:,half:2*half],"g0":fg.at[:,0:half],"g1":fg.at[:,half:2*half],"u0":fu.at[:,0:half],"u1":fu.at[:,half:2*half],
-        "o":fo,"h0":fh0,"h1":fh1}
-    for name,out in outs.items():
-        three,ss,rs=take(3)
-        thirds[name]=Third(seconds[name].two,three,out,ss,rs)
-    pairs={"d":(fd,od),"g":(fg,og),"u":(fu,ou),"o":(fo,oo),"h0":(fh0,oh0),"h1":(fh1,oh1)}
+    ff=2*half
+    fd,fg,fu,fo,fh0,fh1,fq=take(7)
+    outs={"d0":fd.at[:,0:half],"d1":fd.at[:,half:ff],"g0":fg.at[:,0:half],"g1":fg.at[:,half:ff],"u0":fu.at[:,0:half],"u1":fu.at[:,half:ff],
+        "o":fo,"h0":fh0,"h1a":fh1.at[:,0:256],"h1b":fh1.at[:,256:ga1.shape[-1]]}
+    firsts,seconds,thirds={},{},{}
+    ones={"d0":d0,"d1":d1}
+    for name,src,first in (("g0",gg.at[:,:,:,:,0:half],"y"),("g1",gg.at[:,:,:,:,half:ff],"x"),("u0",gu.at[:,:,:,:,0:half],"y"),("u1",gu.at[:,:,:,:,half:ff],"x"),
+            ("o",gow,"y"),("h0",ga0,"y"),("h1a",ga1.at[:,:,:,:,0:256],"y"),("h1b",ga1.at[:,:,:,:,256:ga1.shape[-1]],"y")):
+        ones[name],sem=take(2)
+        firsts[name]=First(src,ones[name],sem,first)
+    for name in ("h1a","h1b"):
+        two,three,ss,rs,came,sem=take(6)
+        seconds[name]=SecondZ(ones[name],two,three,ss,rs)
+        thirds[name]=ThirdX(two,came,outs[name],sem)
+    for name in ("d0","d1","g0","g1","u0","u1","o","h0"):
+        two,sem,three,ss,rs=take(5)
+        seconds[name]=Second(ones[name],two,sem,"x" if name in ("g1","u1") else "y")
+        thirds[name]=Third(two,three,outs[name],ss,rs)
+    pairs={}
+    at=0
+    for name,ref in (("g",fg),("u",fu),("d",fd),("q",fq),("o",fo)):
+        pairs[name]=(ref,grads.at[:,at:at+ref.shape[-1]])
+        at+=ref.shape[-1]
     finals={k:remote(a,b,fin_s.at[i],fin_r.at[i],diag) for i,(k,(a,b)) in enumerate(pairs.items())}
     def give(*names):
         @pl.when(own)
@@ -399,7 +514,8 @@
             for k in names.split(): getattr(group[k],what)()
     run((seconds,"start","d0 d1"))
     loads[1].wait(); loads[2].wait()
-    run((firsts,"start","g0 u0 g1 u1"))
+    loads[3].wait()
+    run((firsts,"start","g0 g1 u0 o"))
     heads=cols//HD; P_=heads//2
     for p in range(P_):
         q_t[p]=q_s[p].T
@@ -411,7 +527,7 @@
             r=slice(half_*64,half_*64+64)
             dd[2*p+half_:2*p+half_+1,:]=jnp.sum(dm_t[p,r,:].astype(f32)*dq_t[p,r,:],0,keepdims=True)
     dk_s[...]=jnp.zeros_like(dk_s); dv_s[...]=jnp.zeros_like(dv_s)
-    loads[3].wait(); loads[4].wait(); loads[5].wait()
+    loads[4].wait(); loads[5].wait()
     sc=HD**-0.5
     width=tok_t.shape[0]; quarter=width//4; hp=P_*128; part=hp//2
     def raw_grads(half_):
@@ -438,11 +554,13 @@
     def middle():
         raw_grads(0)
         weight_grads(0)
-    events={1:[lambda: run((seconds,"finish","d0 d1"),(thirds,"start","d0 d1"),(firsts,"finish","g0"),(seconds,"start","g0"))],
-        3:[lambda: run((firsts,"finish","u0 g1"),(seconds,"start","u0 g1"),(firsts,"start","o")),middle,lambda: run((firsts,"start","h0"))],
-        4:[lambda: run((thirds,"finish","d0 d1")),lambda: give("d"),lambda: run((seconds,"finish","g0"),(thirds,"start","g0"))],
-        5:[lambda: run((firsts,"finish","u1"),(seconds,"start","u1"),(seconds,"finish","u0"),(thirds,"start","u0"))],
-        6:[lambda: run((seconds,"finish","g1"),(thirds,"start","g1"))]}
+    events={0:[lambda: run((seconds,"finish","d0 d1"),(thirds,"start","d0 d1"),(firsts,"finish","g0"),(seconds,"start","g0"),(firsts,"start","u1"))],
+        2:[lambda: run((firsts,"finish","u0 g1"),(seconds,"start","u0 g1"))],
+        3:[lambda: run((thirds,"finish","d0 d1")),lambda: give("d"),lambda: run((seconds,"finish","g0"),(thirds,"start","g0")),middle,lambda: run((firsts,"start","h0"))],
+        4:[lambda: run((seconds,"finish","g1"),(thirds,"start","g1"),(firsts,"finish","o"),(seconds,"start","o"))],
+        5:[lambda: run((firsts,"finish","u1"),(seconds,"start","u1"),(thirds,"finish","g0 g1")),lambda: give("g")],
+        6:[lambda: run((seconds,"finish","u0"),(thirds,"start","u0"))],
+        7:[lambda: run((firsts,"finish","h0"),(seconds,"start","h0"),(seconds,"finish","o"),(thirds,"start","o"))]}
     def body(h,_):
         for i in range(n//QB):
             bwd_head(h,i,q_t,q_s,k_s,k_t,v_s,dm_t,dm,lse,dd,start,dq_t,dk_s,dv_s)
@@ -455,8 +573,8 @@
     raw_grads(1)
     nb=n//QB
     def cross(b): return remote(term.at[b],other.at[b],core_s.at[b],core_r.at[b],{"c":1-c})
-    def far(b): return remote(summed.at[b],gtok.at[b],far_s.at[b],far_r.at[b],diag)
-    def near(b): return pltpu.make_async_copy(summed.at[b],gtok.at[b],far_r.at[b])
+    def far(b): return remote(term.at[b],gtok.at[b],far_s.at[b],far_r.at[b],diag)
+    def near(b): return pltpu.make_async_copy(term.at[b],gtok.at[b],far_r.at[b])
     def fetch(b): return pltpu.make_async_copy(d_one.at[b],d_buf.at[lax.rem(b,2)],d_sem.at[lax.rem(b,2)])
     fetch(0).start(); fetch(1).start()
     def make(b,_):
@@ -466,11 +584,11 @@
         cross(b).start()
         return 0
     lax.fori_loop(0,nb,make,0)
-    run((seconds,"finish","u1"),(thirds,"start","u1"),(firsts,"finish","o"),(seconds,"start","o"))
     def total(b,_):
         cross(b).wait_recv()
+        cross(b).wait_send()
         fetch(b).wait()
-        summed[b]=(d_buf[lax.rem(b,2)]+(term[b].astype(f32)+other[b].astype(f32))).astype(bf)
+        term[b]=(d_buf[lax.rem(b,2)]+(term[b].astype(f32)+other[b].astype(f32))).astype(bf)
         @pl.when(b+2<nb)
         def _():
             fetch(b+2).start()
@@ -481,25 +599,27 @@
         def _():
             far(b).start()
         return 0
-    lax.fori_loop(0,1,total,0)
+    lax.fori_loop(0,2,total,0)
     weight_grads(1)
-    run((firsts,"start","h1"))
-    lax.fori_loop(1,2,total,0)
-    run((firsts,"finish","h0"),(seconds,"start","h0"),(seconds,"finish","o"),(thirds,"start","o"))
+    run((firsts,"start","h1a h1b"),(seconds,"finish","h0"),(thirds,"start","h0"),(seconds,"finish","u1"),(thirds,"start","u1"))
     lax.fori_loop(2,4,total,0)
-    run((thirds,"finish","g0 g1 u0 u1"))
-    run((firsts,"finish","h1"),(seconds,"start","h1"))
+    run((thirds,"finish","u0 o"))
+    give("o")
+    run((firsts,"finish","h1a"),(seconds,"start","h1a"))
     lax.fori_loop(4,nb,total,0)
-    run((seconds,"finish","h0"),(thirds,"start","h0"),(thirds,"finish","o"))
-    give("g","u","o")
-    run((seconds,"finish","h1"),(thirds,"start","h1"),(thirds,"finish","h0"))
-    give("h0")
-    run((thirds,"finish","h1"))
-    give("h1")
+    run((firsts,"finish","h1b"),(seconds,"start","h1b"),(thirds,"finish","u1 h0"))
+    give("u")
+    hc=cols//2; hw=fh0.shape[-1]
+    rr=lax.broadcasted_iota(jnp.int32,(hw,3*cols),0); cc=lax.broadcasted_iota(jnp.int32,(hw,3*cols),1)
+    jj=cc//cols
+    def sort(half_): return jnp.where((rr==jj*hc+cc-jj*cols-half_*hc)&(cc-jj*cols>=half_*hc)&(cc-jj*cols<(half_+1)*hc),1.0,0.0).astype(bf)
+    low=dot(fh0[...],sort(0)); last_map=sort(1)
+    run((seconds,"finish","h1a"),(thirds,"start","h1a"),(seconds,"finish","h1b"),(thirds,"start","h1b"),(thirds,"finish","h1a h1b"))
+    fq[...]=(low+dot(fh1[...],last_map)).astype(bf)
+    give("q")
     for group in (firsts,seconds,thirds):
         for x in group.values(): x.drain()
     def drain(b,_):
-        cross(b).wait_send()
         @pl.when(own)
         def _():
             near(b).wait()
@@ -527,14 +647,15 @@
     one=lambda k: [vm((4,2,r,k),bf),dma(2)]
     two=lambda k: [vm((4,r,k),bf),dma(2)]
     three=lambda k: [vm((3,r,k),bf),dma(3),dma(3)]
+    by_z=lambda k: [vm((2,r,k),bf),vm((3,2,r,k),bf),dma(3),dma(3),vm((r,k),bf),dma(2)]
     return pl.pallas_call(functools.partial(fused_bwd_kernel,n,cols),
-      out_shape=[S((r,ff),bf)]*3+[S((r,w),bf)]+[S((r,hw),bf)]*2+[S(blocks,bf)],
-      in_specs=[V]*10+[A]*7,out_specs=[V]*6+[A],
+      out_shape=[S((r,3*ff+3*cols+w),bf),S(blocks,bf)],
+      in_specs=[V]*10+[A]*7,out_specs=[V,A],
       scratch_shapes=[vm((pr,128,n),bf)]*3+[vm((pr,128,n),f32),vm((pr,n,128),f32),vm((pr,n,128),f32),vm((heads,n),f32),vm((3,n,pr*128),bf),
-        like(gg),like(gu),like(gow),like(tok_t),like(wt),vm((2,QB,width),f32),vm((4,2,2,r,hw),bf),vm((4,2,2,r,hw),bf)]+[vm(blocks,bf)]*3
-        +[dma(6),dma(2)]+[dma(nb)]*4+[dma(6),dma(6)]
-        +(one(h)+two(h))*4+one(w)+two(w)+(one(hw)+two(hw))*2+two(h)*2
-        +[vm((r,ff),bf)]*3+[vm((r,w),bf)]+[vm((r,hw),bf)]*2+three(h)*6+three(w)+three(hw)*2,
+        like(gg),like(gu),like(gow),like(tok_t),like(wt),vm((2,QB,width),f32),vm((4,2,2,r,hw),bf),vm((4,2,2,r,hw),bf)]+[vm(blocks,bf)]*2
+        +[dma(6),dma(2)]+[dma(nb)]*4+[dma(5),dma(5)]
+        +[vm((r,ff),bf)]*3+[vm((r,w),bf)]+[vm((r,hw),bf)]*2+[vm((r,3*cols),bf)]
+        +one(h)*4+one(w)+one(hw)+one(256)+one(hw-256)+by_z(256)+by_z(hw-256)+(two(h)+three(h))*6+two(w)+three(w)+two(hw)+three(hw),
       compiler_params=pltpu.CompilerParams(vmem_limit_bytes=64<<20,collective_id=1,has_side_effects=True),name="attn_bwd_reduce")(
         q_s,k_s,v_s,dm,lse,start,cos,sin,d0,d1,m_t,gg,gu,gow,tok_t,wt,d_one.reshape(blocks))
 
@@ -702,7 +823,7 @@
         vm(blocks,bf),vm(blocks,bf),vm(blocks,bf),vm(blocks,bf),vm(blocks,bf),vm((16,width),f32),vm((4,2,2,r,ff),bf),
         pltpu.SemaphoreType.DMA,pltpu.SemaphoreType.DMA]+[dma]*8+[pltpu.SemaphoreType.DMA((2,))]*2,
       compiler_params=pltpu.CompilerParams(vmem_limit_bytes=64<<20,collective_id=3,has_side_effects=True),name="ffn")(
-        tok,og.reshape(blocks),mixed,ofull,wg,wu,wd,ga[None],gb[None])
+        tok,og.reshape(blocks),mixed,ofull,wg,wu,wd,ga,gb)
 
 def rms_forward(resid):
     inverse=lax.rsqrt(jnp.mean(resid*resid,-1,keepdims=True)+NORM_EPS)
@@ -728,83 +849,80 @@
     return part.astype(f32)+lax.ppermute(part,"c",CORE).astype(f32)
 
 def on_device(tokens,out_grad,doc_lengths,w_query,w_key,w_value,w_out,gain_one,w_gate,w_up,w_down,gain_two):
-    cols=w_query.shape[1]; ff=w_gate.shape[1]; n,width=tokens.shape
-    quad=lax.axis_size("q")==8 and w_query.shape[0]==48
-    if not quad:
-        own=lax.axis_index("c")==lax.axis_index("m")
-        pick=lambda a: jnp.where(own,a,lax.ppermute(a,"c",CORE))
-        tokens,out_grad,doc_lengths=pick(tokens),pick(out_grad),pick(doc_lengths)
+    cols=w_query.shape[1]; n,width=tokens.shape
+    if lax.axis_size("q")==8 and lax.axis_size("m")==2 and w_query.shape[0]==48:
+        tokens,cos,sin,q,k,v,tok_t,wt,start,gain_a,gain_b,ofull,gate_w,up_w,down_t,m_t,mixed,lse=fused_fwd(
+            doc_lengths,tokens,w_query,w_key,w_value,w_out.T,w_gate,w_up,w_down.T,gain_one,gain_two)
+        ofull,gate_w,up_w,down_t=[a.reshape(width,a.shape[-1]) for a in (ofull,gate_w,up_w,down_t)]
+        output,gg,gu,d_one,dm,gow,*downs=ffn_call(tokens,out_grad,mixed,ofull,gate_w,up_w,down_t,gain_a,gain_b,cols)
+        grads,gtok=fused_bwd(q,k,v,m_t,dm,lse,start,cos,sin,gg,gu,gow,*downs,tok_t,wt,d_one,cols)
+        ff=w_gate.shape[1]
+        got,at=[],0
+        for wide in (ff,ff,ff,cols,cols,cols,128,cols):
+            got.append(grads[:,at:at+wide].astype(f32))
+            at+=wide
+        sgate,sup,sdown,sq,sk,sv,sgain,sout=got
+        return (output.reshape(n,width),gtok.astype(f32).reshape(n,width),sq,sk,sv,sout.T,sgain[:,0],sgate,sup,sdown.T,sgain[:,1])
+    own=lax.axis_index("c")==lax.axis_index("m")
+    pick=lambda a: jnp.where(own,a,lax.ppermute(a,"c",CORE))
+    tokens,out_grad,doc_lengths=pick(tokens),pick(out_grad),pick(doc_lengths)
     start=doc_starts(doc_lengths[0],n)
     cos,sin=rope_tables(jnp.arange(n,dtype=jnp.int32)-start)
     start=start[None]
+    ff=w_gate.shape[1]
     cast=lambda a: a.astype(bf)
     gains=jnp.pad(jnp.stack([cast(gain_one),cast(gain_two)],1),((0,0),(0,126)))
     apack=jnp.concatenate([cast(w_query),cast(w_key),cast(w_value),gains],1)
     def gather(a):
         return lax.all_gather(lax.ppermute(a,("c","m"),DIAG),("q","m"),axis=0,tiled=True)
-    if quad:
-        tokens,cos,sin,start,afull,ofull,gate_w,up_w,down_t,q,k,v,m_t,mixed,lse,tok_t,wt=fused_fwd(
-            tokens,cos,sin,start,apack,cast(w_out).T,cast(w_gate),cast(w_up),cast(w_down).T,cols)
-        afull,ofull,gate_w,up_w,down_t=[a.reshape(width,a.shape[-1]) for a in (afull,ofull,gate_w,up_w,down_t)]
-    else:
-        afull,ofull,gate_w,up_w,down_t=[gather(a) for a in (apack,cast(w_out).T,cast(w_gate),cast(w_up),cast(w_down).T)]
-        q,k,v,m_t,mixed,lse=attn_fwd(tokens,afull[:,:3*cols],cos,sin,start)
-    hp=cols//HD*64
-    put=spread(hp,cols,False)
+    afull,ofull,gate_w,up_w,down_t=[gather(a) for a in (apack,cast(w_out).T,cast(w_gate),cast(w_up),cast(w_down).T)]
+    q,k,v,m_t,mixed,lse=attn_fwd(tokens,afull[:,:3*cols],cos,sin,start)
+    put=spread(cols//HD*64,cols,False)
     out_t=dot_nt(ofull,put).astype(bf)
     gain_a=afull[:,3*cols].astype(f32); gain_b=afull[:,3*cols+1].astype(f32)
-    own=lax.axis_index("c")==lax.axis_index("m")
-    if quad:
-        output,gg,gu,d_one,dm,gow,*downs=ffn_call(tokens,out_grad,mixed,ofull,gate_w,up_w,down_t,gain_a,gain_b,cols)
-        output=output.reshape(n,width)
-        sdown,sgate,sup,sout,sh0,sh1,gtok=[a.astype(f32) for a in fused_bwd(q,k,v,m_t,dm,lse,start,cos,sin,gg,gu,gow,*downs,tok_t,wt,d_one,cols)]
-        hc=cols//2
-        sq,sk,sv=[jnp.concatenate([a[:,j*hc:(j+1)*hc] for a in (sh0,sh1)],1) for j in range(3)]
-        return (output,gtok.reshape(n,width),sq,sk,sv,sout[:,128:].T,sout[:,0],sgate,sup,sdown.T,sout[:,1])
-    else:
-        attn=core_sum(dot_nt(mixed,out_t).astype(bf))
-        normed_one,inv_one=rms_forward(tokens.astype(f32)+attn)
-        hidden=normed_one*gain_a
-        hb=hidden.astype(bf)
-        gate=dot(hb,gate_w); up=dot(hb,up_w)
-        sg=jax.nn.sigmoid(gate)
-        act=(gate*sg*up).astype(bf)
-        ffn=core_sum(dot_nt(act,down_t).astype(bf))
-        normed_two,inv_two=rms_forward(hidden+ffn)
-        output=(normed_two*gain_b).astype(bf)
-        g=out_grad.astype(f32)
-        g_gain_two=jnp.sum(g*normed_two,0)
-        d_two=rms_backward(g*gain_b,normed_two,inv_two)
-        d_ffn=d_two.astype(bf)
-        tn=lambda a,b: lax.dot_general(a,b,(((0,),(0,)),((),())),preferred_element_type=f32)
-        d_act=dot(d_ffn,down_t)
-        d_up=(d_act*gate*sg).astype(bf)
-        d_gate=(d_act*up*sg*(1.0+gate*(1.0-sg))).astype(bf)
-        hterm=(dot_nt(d_gate,gate_w)+dot_nt(d_up,up_w)).astype(bf)
-        gff=[tn(hb,d_gate).astype(bf),tn(hb,d_up).astype(bf),tn(d_ffn,act).astype(bf)]
-        d_hidden=d_two+core_sum(hterm)
-        g_gain_one=jnp.sum(d_hidden*normed_one,0)
-        d_one=rms_backward(d_hidden*gain_a,normed_one,inv_one)
-        d_attn=d_one.astype(bf)
-        dm=dot(d_attn,out_t).astype(bf)
-        output=jnp.where(own,output,lax.ppermute(output,("c","m"),[(1,2),(2,1)]))
-
-        ggain=jnp.pad(jnp.stack([g_gain_one,g_gain_two],1),((0,0),(0,126))).astype(bf)
-        dqkv=attn_bwd(q,k,v,m_t,dm,lse,start,cos,sin)
-        term=0.0; gqkv=[]
-        for j in range(3):
-            wp=dot_nt(afull[:,j*cols:(j+1)*cols],put).astype(bf)
-            term=term+dot_nt(dqkv[j],wp)
-            gqkv.append(dot(tn(tokens,dqkv[j]).astype(bf),put).astype(bf))
-        gtok=(d_one+core_sum(term.astype(bf))).astype(bf)
-        gtok=lax.ppermute(gtok,("c","m"),DIAG).astype(f32)
-        g_out=dot(tn(d_attn,mixed).astype(bf),put).astype(bf)
-        gatt=jnp.concatenate([ggain,g_out]+gqkv,1)
-        add=lambda a: lax.psum_scatter(a,("q","m"),scatter_dimension=0,tiled=True)
-        sff,sat=[add(a) for a in gff],add(gatt)
-        sff,sat=lax.ppermute(jnp.concatenate(sff,1),("c","m"),DIAG).astype(f32),lax.ppermute(sat,("c","m"),DIAG).astype(f32)
-        piece=lambda j: sat[:,128+j*cols:128+(j+1)*cols]
-        return (output,gtok,piece(1),piece(2),piece(3),piece(0).T,sat[:,0],sff[:,:ff],sff[:,ff:2*ff],sff[:,2*ff:].T,sat[:,1])
+    attn=core_sum(dot_nt(mixed,out_t).astype(bf))
+    normed_one,inv_one=rms_forward(tokens.astype(f32)+attn)
+    hidden=normed_one*gain_a
+    hb=hidden.astype(bf)
+    gate=dot(hb,gate_w); up=dot(hb,up_w)
+    sg=jax.nn.sigmoid(gate)
+    act=(gate*sg*up).astype(bf)
+    ffn=core_sum(dot_nt(act,down_t).astype(bf))
+    normed_two,inv_two=rms_forward(hidden+ffn)
+    output=(normed_two*gain_b).astype(bf)
+    g=out_grad.astype(f32)
+    g_gain_two=jnp.sum(g*normed_two,0)
+    d_two=rms_backward(g*gain_b,normed_two,inv_two)
+    d_ffn=d_two.astype(bf)
+    tn=lambda a,b: lax.dot_general(a,b,(((0,),(0,)),((),())),preferred_element_type=f32)
+    d_act=dot(d_ffn,down_t)
+    d_up=(d_act*gate*sg).astype(bf)
+    d_gate=(d_act*up*sg*(1.0+gate*(1.0-sg))).astype(bf)
+    hterm=(dot_nt(d_gate,gate_w)+dot_nt(d_up,up_w)).astype(bf)
+    gff=[tn(hb,d_gate).astype(bf),tn(hb,d_up).astype(bf),tn(d_ffn,act).astype(bf)]
+    d_hidden=d_two+core_sum(hterm)
+    g_gain_one=jnp.sum(d_hidden*normed_one,0)
+    d_one=rms_backward(d_hidden*gain_a,normed_one,inv_one)
+    d_attn=d_one.astype(bf)
+    dm=dot(d_attn,out_t).astype(bf)
+    output=jnp.where(own,output,lax.ppermute(output,("c","m"),[(1,2),(2,1)]))
+
+    ggain=jnp.pad(jnp.stack([g_gain_one,g_gain_two],1),((0,0),(0,126))).astype(bf)
+    dqkv=attn_bwd(q,k,v,m_t,dm,lse,start,cos,sin)
+    term=0.0; gqkv=[]
+    for j in range(3):
+        wp=dot_nt(afull[:,j*cols:(j+1)*cols],put).astype(bf)
+        term=term+dot_nt(dqkv[j],wp)
+        gqkv.append(dot(tn(tokens,dqkv[j]).astype(bf),put).astype(bf))
+    gtok=(d_one+core_sum(term.astype(bf))).astype(bf)
+    gtok=lax.ppermute(gtok,("c","m"),DIAG).astype(f32)
+    g_out=dot(tn(d_attn,mixed).astype(bf),put).astype(bf)
+    gatt=jnp.concatenate([ggain,g_out]+gqkv,1)
+    add=lambda a: lax.psum_scatter(a,("q","m"),scatter_dimension=0,tiled=True)
+    sff,sat=[add(a) for a in gff],add(gatt)
+    sff,sat=lax.ppermute(jnp.concatenate(sff,1),("c","m"),DIAG).astype(f32),lax.ppermute(sat,("c","m"),DIAG).astype(f32)
+    piece=lambda j: sat[:,128+j*cols:128+(j+1)*cols]
+    return (output,gtok,piece(1),piece(2),piece(3),piece(0).T,sat[:,0],sff[:,:ff],sff[:,ff:2*ff],sff[:,2*ff:].T,sat[:,1])
 
 def solution(mesh):
     dp,mp=mesh.shape["dp"],mesh.shape["mp"]

time: 319 us -> 294 us (0.922); the launches traced: 319 us -> 289 us
  other arithmetic: 28.4 us -> 8.5 us
  local copies, waits for them, and re-layouts: 7.36 us -> 2.11 us
    convert_element_type x11 -> x1, other arithmetic: 11.9 us -> 0.71 us  [on_device(): got.append(grads[:, at:at + wide].astype(f32))]
    slice x5 -> x1, local copies, waits for them, and re-layouts: 4.98 us -> 0.7 us  [on_device(): sgain[:, 1]]
    sin x1 -> x0, other arithmetic: 4.26 us -> none  [rope_tables(): return (jnp.cos(a), jnp.sin(a))]
where the time goes in v2:
time: 294 us; the launch traced here: 289 us
  Pallas kernels  277 us (94%)
  other arithmetic  8.5 us (3%)
    pallas_call x1, Pallas kernels, fused_bwd(): pl.pallas_call(functools.partial(fused_bwd_kernel, n, cols), out_shape=[S...  106 us
    pallas_call x1, Pallas kernels, fused_fwd(): pl.pallas_call(functools.partial(fused_fwd_kernel, n, cols), out_shape=[S...  104 us
    pallas_call x1, Pallas kernels, ffn_call(): pl.pallas_call(functools.partial(ffn_kernel, n, cols), out_shape=[S(block...  67.1 us

profile of v2, /device:TPU:1, one launch (start us, length us, event | category | flops | bytes accessed | tf_op | source)
XLA Modules:
  0.0 288.9 jit_solution(8716352287406879723)
XLA Ops:
  0.6 104.2 %attn_fwd_gather.1 = (bf16[1536,768]{1,0:T(8,128)(2,1)}, f32[1536,128]{1,0:T(8,128)}, f32[1536,128]{1,0:T(8,128)}, bf16[4,1536,128]{2,1,0:T(8,128)(2,1)}, bf16[4...) custom-call(s32[1,4]{1,0:T(1,128)} %lengths.1, ...), custom_call_target="tpu_custom_call" | custom-call | tf_op jit(solution)/shard_map/attn_fwd_gather/pallas_call | solution.py:456
  104.8 67.1 %ffn.1 = (bf16[6,256,768]{2,1,0:T(8,128)(2,1)}, bf16[4,2,2,48,1280]{4,3,2,1,0:T(8,128)(2,1)}, bf16[4,2,2,48,1280]{4,3,2,1,0:T(8,128)(2,1)}, f32[1536,768]{1,0:T(...) custom-call(bf16[1536,768]{1,0:T(8,128)(2,1)} %get-tuple-element.39., ...), custom_call_target="tpu_custom_call" | custom-call | tf_op jit(solution)/shard_map/ffn/pallas_call | solution.py:819
  171.9 106.1 %attn_bwd_reduce.1 = (bf16[48,5504]{1,0:T(8,128)(2,1)}, bf16[6,256,768]{2,1,0:T(8,128)(2,1)}) custom-call(bf16[4,1536,128]{2,1,0:T(8,128)(2,1)} %get-tuple-element.48.q_s, bf16[4,1536,128]{2,1,0:T(8,128)(2,1)} %get-tuple-element.49.k_s, bf16[4,1536,128]{2,1,0:T(8,128)(2,1)} %get-tuple-element.50.v_s, bf16[4,1536,128]{2,1,0:T(8,128)(2,1)} %get-tuple-element.51.dm, ...), custom_call_target="tpu_custom_call" | custom-call | tf_op jit(solution)/shard_map/attn_bwd_reduce/pallas_call | solution.py:651
  278.1 0.7 slice_convert_fusion.5
  278.8 0.7 slice_reduce_fusion
  279.5 1.5 convert_bitcast_fusion.1
  281.0 1.9 convert_bitcast_fusion
  282.9 0.0 copy-start
  282.9 4.4 %bitcast_convert_fusion = f32[1536,768]{1,0:T(8,128)} fusion(bf16[6,256,768]{2,1,0:T(8,128)(2,1)} %get-tuple-element.65), kind=kLoop, calls=%fused_computation | loop fusion | flops 1179648 | bytes 7077888 | tf_op jit(solution)/shard_map/reshape | solution.py:865
  287.3 0.0 copy-done
  287.3 1.4 copy.25
Async XLA Ops:
  282.9 4.4 %copy-start = (bf16[6,256,768]{2,1,0:T(8,128)(2,1)S(1)}, bf16[6,256,768]{2,1,0:T(8,128)(2,1)}, u32[]{:S(2)}) copy-start(bf16[6,256,768]{2,1,0:T(8,128)(2,1)} %get-tuple-element.47) | copy-start | bytes 7077892

commit v3 on v2

--- a/solution.py
+++ b/solution.py
@@ -464,13 +464,13 @@
       compiler_params=pltpu.CompilerParams(vmem_limit_bytes=60<<20,collective_id=0,has_side_effects=True),name="attn_fwd_gather")(
         lengths,jnp.asarray(freq),tok,wq,wk,wv,w_out,wg,wu,wd,g1[None],g2[None])
 
-def fused_bwd_kernel(n,cols,q_s,k_s,v_s,dm,lse,start,cos,sin,d0,d1,m_i,g_i,u_i,o_i,tok_i,wt_i,d_one,grads,gtok,
-        q_t,k_t,dm_t,dq_t,dk_s,dv_s,dd,dqkv,gg,gu,gow,tok_t,wt,d_buf,ga0,ga1,term,other,load_s,d_sem,core_s,core_r,far_s,far_r,fin_s,fin_r,*scr):
+def fused_bwd_kernel(n,cols,lse,start,q_i,k_i,v_i,dm_i,cos_i,sin_i,d0_i,d1_i,m_i,g_i,u_i,o_i,tok_i,wt_i,d_one,grads,gtok,
+        q_t,k_t,dm_t,dq_t,dk_s,dv_s,dd,dqkv,gg,gu,gow,tok_t,wt,d_buf,ga0,ga1,term,other,q_s,k_s,v_s,dm,cos,sin,d0,d1,load_s,d_sem,core_s,core_r,far_s,far_r,fin_s,fin_r,*scr):
     z,y,m=place(); c=lax.axis_index("c")
     own=c==m
     diag={"c":1-c,"m":1-m}
-    loads=[pltpu.make_async_copy(a,b,load_s.at[i]) for i,(a,b) in enumerate(((m_i,dq_t),(g_i,gg),(u_i,gu),(o_i,gow),(tok_i,tok_t),(wt_i,wt)))]
-    for x in loads: x.start()
+    loads=[pltpu.make_async_copy(a,b,load_s.at[i]) for i,(a,b) in enumerate(((m_i,dq_t),(g_i,gg),(u_i,gu),(o_i,gow),(tok_i,tok_t),(wt_i,wt),(d0_i,d0),(d1_i,d1),(q_i,q_s),(k_i,k_s),(dm_i,dm),(v_i,v_s),(cos_i,cos),(sin_i,sin)))]
+    for i in (6,7,1,8,9,10,2,3,0,11,12,13,4,5): loads[i].start()
     greet(peers(z,y,m)+both(c,m))
     scr=list(scr)
     def take(k):
@@ -512,22 +512,25 @@
     def run(*steps):
         for group,what,names in steps:
             for k in names.split(): getattr(group[k],what)()
+    loads[6].wait(); loads[7].wait()
     run((seconds,"start","d0 d1"))
-    loads[1].wait(); loads[2].wait()
-    loads[3].wait()
-    run((firsts,"start","g0 g1 u0 o"))
+    loads[1].wait()
+    run((firsts,"start","g0 g1"))
+    for i in (8,9,10): loads[i].wait()
     heads=cols//HD; P_=heads//2
     for p in range(P_):
         q_t[p]=q_s[p].T
         k_t[p]=k_s[p].T
         dm_t[p]=dm[p].T
+    loads[2].wait(); loads[3].wait()
+    run((firsts,"start","u0 o"))
     loads[0].wait()
     for p in range(P_):
         for half_ in range(2):
             r=slice(half_*64,half_*64+64)
             dd[2*p+half_:2*p+half_+1,:]=jnp.sum(dm_t[p,r,:].astype(f32)*dq_t[p,r,:],0,keepdims=True)
     dk_s[...]=jnp.zeros_like(dk_s); dv_s[...]=jnp.zeros_like(dv_s)
-    loads[4].wait(); loads[5].wait()
+    for i in (4,5,11,12,13): loads[i].wait()
     sc=HD**-0.5
     width=tok_t.shape[0]; quarter=width//4; hp=P_*128; part=hp//2
     def raw_grads(half_):
@@ -650,14 +653,14 @@
     by_z=lambda k: [vm((2,r,k),bf),vm((3,2,r,k),bf),dma(3),dma(3),vm((r,k),bf),dma(2)]
     return pl.pallas_call(functools.partial(fused_bwd_kernel,n,cols),
       out_shape=[S((r,3*ff+3*cols+w),bf),S(blocks,bf)],
-      in_specs=[V]*10+[A]*7,out_specs=[V,A],
+      in_specs=[V,V]+[A]*15,out_specs=[V,A],
       scratch_shapes=[vm((pr,128,n),bf)]*3+[vm((pr,128,n),f32),vm((pr,n,128),f32),vm((pr,n,128),f32),vm((heads,n),f32),vm((3,n,pr*128),bf),
         like(gg),like(gu),like(gow),like(tok_t),like(wt),vm((2,QB,width),f32),vm((4,2,2,r,hw),bf),vm((4,2,2,r,hw),bf)]+[vm(blocks,bf)]*2
-        +[dma(6),dma(2)]+[dma(nb)]*4+[dma(5),dma(5)]
+        +[like(a) for a in (q_s,k_s,v_s,dm,cos,sin,d0,d1)]+[dma(14),dma(2)]+[dma(nb)]*4+[dma(5),dma(5)]
         +[vm((r,ff),bf)]*3+[vm((r,w),bf)]+[vm((r,hw),bf)]*2+[vm((r,3*cols),bf)]
         +one(h)*4+one(w)+one(hw)+one(256)+one(hw-256)+by_z(256)+by_z(hw-256)+(two(h)+three(h))*6+two(w)+three(w)+two(hw)+three(hw),
       compiler_params=pltpu.CompilerParams(vmem_limit_bytes=64<<20,collective_id=1,has_side_effects=True),name="attn_bwd_reduce")(
-        q_s,k_s,v_s,dm,lse,start,cos,sin,d0,d1,m_t,gg,gu,gow,tok_t,wt,d_one.reshape(blocks))
+        lse,start,q_s,k_s,v_s,dm,cos,sin,d0,d1,m_t,gg,gu,gow,tok_t,wt,d_one.reshape(blocks))
 
 def dot_nt_t(a,b,put):
     return dot(dot(a,b).astype(bf),put).astype(bf)
@@ -677,10 +680,12 @@
 def norm_back(e,nrm,inv):
     return inv*(e-nrm*jnp.mean(e*nrm,-1,keepdims=True))
 
-def ffn_kernel(n,cols,tok,og,mixed,ofull,wg,wu,wd,ga,gb,output,gg,gu,d_one,dm,gow,one0,one1,
-        out_t,t1,t2,act,normed,inv1,hb_t,dff_t,part,oa,of,oh,summed,gsum,gd,og_s,og_r,a_s,a_r,f_s,f_r,h_s,h_r,x_s,x_r,s0,s1):
+def ffn_kernel(n,cols,tok_i,og,mixed,ofull,wg_i,wu_i,wd_i,ga,gb,output,gg_o,gu_o,d_one_o,dm,gow,one0,one1,
+        out_t,t1,t2,act,normed,inv1,hb_t,dff_t,part,oa,of,oh,summed,gsum,gd,og_s,og_r,a_s,a_r,f_s,f_r,h_s,h_r,x_s,x_r,s0,s1,tok,wg,wu,wd,gg,gu,d_one,load_s,keep_s,d_s):
     z,y,m=place(); c=lax.axis_index("c")
     own=c==m
+    loads=[pltpu.make_async_copy(a,b,load_s.at[i]) for i,(a,b) in enumerate(((tok_i,tok),(wg_i,wg),(wu_i,wu),(wd_i,wd)))]
+    for x in loads: x.start()
     greet(peers(z,y,m)+both(c,m))
     nb=n//QB
     grad_far=pltpu.make_async_remote_copy(src_ref=og,dst_ref=summed,send_sem=og_s,recv_sem=og_r,device_id={"c":1-c},device_id_type=MESH)
@@ -699,6 +704,7 @@
     def _():
         grad_far.start()
         grad_near.start()
+    for x in loads: x.wait()
     def forward(b,_):
         rows=rows_of(b)
         ca(b).wait_recv()
@@ -773,6 +779,9 @@
         gu[i]=dot(hb_t[rows4(i),:],t2[...]).astype(bf).reshape(2,2,quarter//4,ff)
         return 0
     lax.fori_loop(0,4,grads,0)
+    keep=[pltpu.make_async_copy(a,b,keep_s.at[i]) for i,(a,b) in enumerate(((gg,gg_o),(gu,gu_o)))]
+    for x in keep: x.start()
+    def keep_d(b): return pltpu.make_async_copy(d_one.at[rows_of(b)],d_one_o.at[rows_of(b)],d_s.at[b])
     def last(b,_):
         rows=rows_of(b)
         ch(b).wait_recv()
@@ -781,6 +790,7 @@
         gsum[0:8,:]+=fold(dh*nrm)
         d1=norm_back(dh*ga[...],nrm,inv1[rows,:])
         d_one[rows,:]=d1
+        keep_d(b).start()
         da=d1.astype(bf)
         hb_t[:,rows]=da.T
         back=dot(da,out_t[...]).astype(bf)
@@ -797,8 +807,10 @@
     gow[:,:,:,:,0:128]=both_gains.T.astype(bf).reshape(4,2,2,quarter//4,128)
     for x in ch2: x.finish()
     for x in ch2: x.drain()
+    for x in keep: x.wait()
     def drain(b,_):
         ch(b).wait_send()
+        keep_d(b).wait()
         @pl.when(own)
         def _():
             near(b).wait()
@@ -818,10 +830,10 @@
     vm=pltpu.VMEM
     return pl.pallas_call(functools.partial(ffn_kernel,n,cols),
       out_shape=[S(blocks,bf)]+[S((4,2,2,r,ff),bf)]*2+[S((n,width),f32),S((hp//128,n,128),bf),S((4,2,2,r,cols+128),bf)]+[S((4,2,r,ff//2),bf)]*2,
-      in_specs=[V,A]+[V]*7,out_specs=[A]+[V]*7,
+      in_specs=[A,A,V,V,A,A,A,V,V],out_specs=[A,A,A,A]+[V]*4,
       scratch_shapes=[vm((width,hp),bf),vm((n,ff),bf),vm((n,ff),bf),vm((n,ff),bf),vm((n,width),f32),vm((n,1),f32),vm((width,n),bf),vm((width,n),bf),
         vm(blocks,bf),vm(blocks,bf),vm(blocks,bf),vm(blocks,bf),vm(blocks,bf),vm((16,width),f32),vm((4,2,2,r,ff),bf),
-        pltpu.SemaphoreType.DMA,pltpu.SemaphoreType.DMA]+[dma]*8+[pltpu.SemaphoreType.DMA((2,))]*2,
+        pltpu.SemaphoreType.DMA,pltpu.SemaphoreType.DMA]+[dma]*8+[pltpu.SemaphoreType.DMA((2,))]*2+[vm((n,width),bf),vm((width,ff),bf),vm((width,ff),bf),vm((width,ff),bf),vm((4,2,2,r,ff),bf),vm((4,2,2,r,ff),bf),vm((n,width),f32),pltpu.SemaphoreType.DMA((4,)),pltpu.SemaphoreType.DMA((2,)),dma],
       compiler_params=pltpu.CompilerParams(vmem_limit_bytes=64<<20,collective_id=3,has_side_effects=True),name="ffn")(
         tok,og.reshape(blocks),mixed,ofull,wg,wu,wd,ga,gb)
 
@@ -856,13 +868,8 @@
         ofull,gate_w,up_w,down_t=[a.reshape(width,a.shape[-1]) for a in (ofull,gate_w,up_w,down_t)]
         output,gg,gu,d_one,dm,gow,*downs=ffn_call(tokens,out_grad,mixed,ofull,gate_w,up_w,down_t,gain_a,gain_b,cols)
         grads,gtok=fused_bwd(q,k,v,m_t,dm,lse,start,cos,sin,gg,gu,gow,*downs,tok_t,wt,d_one,cols)
-        ff=w_gate.shape[1]
-        got,at=[],0
-        for wide in (ff,ff,ff,cols,cols,cols,128,cols):
-            got.append(grads[:,at:at+wide].astype(f32))
-            at+=wide
-        sgate,sup,sdown,sq,sk,sv,sgain,sout=got
-        return (output.reshape(n,width),gtok.astype(f32).reshape(n,width),sq,sk,sv,sout.T,sgain[:,0],sgate,sup,sdown.T,sgain[:,1])
+        gtok,sgate,sup,sdown,sq,sk,sv,sout,sgain=finish(gtok,grads,cols,w_gate.shape[1])
+        return (output.reshape(n,width),gtok.reshape(n,width),sq,sk,sv,sout.T,sgain[0],sgate,sup,sdown.T,sgain[1])
     own=lax.axis_index("c")==lax.axis_index("m")
     pick=lambda a: jnp.where(own,a,lax.ppermute(a,"c",CORE))
     tokens,out_grad,doc_lengths=pick(tokens),pick(out_grad),pick(doc_lengths)
@@ -924,6 +931,28 @@
     piece=lambda j: sat[:,128+j*cols:128+(j+1)*cols]
     return (output,gtok,piece(1),piece(2),piece(3),piece(0).T,sat[:,0],sff[:,:ff],sff[:,ff:2*ff],sff[:,2*ff:].T,sat[:,1])
 
+def finish_kernel(cols,ff,gtok,grads,gtok_o,g_o,u_o,d_o,q_o,k_o,v_o,w_o,gain_o):
+    gtok_o[...]=gtok[...].astype(f32)
+    @pl.when(pl.program_id(0)==0)
+    def _():
+        at=0
+        for ref,wide in ((g_o,ff),(u_o,ff),(d_o,ff),(q_o,cols),(k_o,cols),(v_o,cols)):
+            ref[...]=grads[:,at:at+wide].astype(f32)
+            at+=wide
+        gain_o[...]=grads[:,at:at+128].astype(f32).T[0:8,:]
+        w_o[...]=grads[:,at+128:].astype(f32)
+
+def finish(gtok,grads,cols,ff):
+    nb,rows,width=gtok.shape; r=grads.shape[0]
+    S=jax.ShapeDtypeStruct
+    block=pl.BlockSpec((1,rows,width),lambda i:(i,0,0))
+    whole=lambda a,b: pl.BlockSpec((a,b),lambda i:(0,0))
+    shapes=[(r,ff)]*3+[(r,cols)]*4+[(8,r)]
+    return pl.pallas_call(functools.partial(finish_kernel,cols,ff),grid=(nb,),
+      out_shape=[S(gtok.shape,f32)]+[S(a,f32) for a in shapes],
+      in_specs=[block,whole(*grads.shape)],out_specs=[block]+[whole(*a) for a in shapes],
+      compiler_params=pltpu.CompilerParams(vmem_limit_bytes=63<<20),name="finish")(gtok,grads)
+
 def solution(mesh):
     dp,mp=mesh.shape["dp"],mesh.shape["mp"]
     fine=Mesh(mesh.devices.reshape(dp//2,2,mp),("q","c","m"))

time: 294 us -> 293 us (level); the launches traced: 289 us -> 295 us
  Pallas kernels: 277 us -> 290 us
  other arithmetic: 8.5 us -> 0 us
    pallas_call x1, Pallas kernels: 67.1 us -> 76.1 us  [ffn_call(): pl.pallas_call(functools.partial(ffn_kernel, n, cols), out_shape=[S(block...]
    pallas_call x0 -> x1, Pallas kernels: none -> 5.86 us  [finish(): pl.pallas_call(functools.partial(finish_kernel, cols, ff), grid=(nb,), ou...]
    reshape x1 -> x0, other arithmetic: 4.36 us -> none  [on_device(): gtok.astype(f32).reshape(n, width)]
    transpose x2 -> x0, other arithmetic: 3.43 us -> none  [on_device(): return (output.reshape(n, width), gtok.astype(f32).reshape(n, width), sq,...]
where the time goes in v3:
time: 293 us; the launch traced here: 295 us
  Pallas kernels  290 us (99%)
  local copies, waits for them, and re-layouts  4.5 us (2%)
    pallas_call x1, Pallas kernels, fused_fwd(): pl.pallas_call(functools.partial(fused_fwd_kernel, n, cols), out_shape=[S...  104 us
    pallas_call x1, Pallas kernels, fused_bwd(): pl.pallas_call(functools.partial(fused_bwd_kernel, n, cols), out_shape=[S...  104 us
    pallas_call x1, Pallas kernels, ffn_call(): pl.pallas_call(functools.partial(ffn_kernel, n, cols), out_shape=[S(block...  76.1 us

profile of v3, /device:TPU:1, one launch (start us, length us, event | category | flops | bytes accessed | tf_op | source)
XLA Modules:
  0.0 295.3 jit_solution(1153510383962954833)
XLA Ops:
  0.6 104.1 %attn_fwd_gather.1 = (bf16[1536,768]{1,0:T(8,128)(2,1)}, f32[1536,128]{1,0:T(8,128)}, f32[1536,128]{1,0:T(8,128)}, bf16[4,1536,128]{2,1,0:T(8,128)(2,1)}, bf16[4...) custom-call(s32[1,4]{1,0:T(1,128)} %lengths.1, ...), custom_call_target="tpu_custom_call" | custom-call | tf_op jit(solution)/shard_map/attn_fwd_gather/pallas_call | solution.py:456
  104.8 76.1 %ffn.1 = (bf16[6,256,768]{2,1,0:T(8,128)(2,1)}, bf16[4,2,2,48,1280]{4,3,2,1,0:T(8,128)(2,1)}, bf16[4,2,2,48,1280]{4,3,2,1,0:T(8,128)(2,1)}, f32[1536,768]{1,0:T(...) custom-call(bf16[1536,768]{1,0:T(8,128)(2,1)} %get-tuple-element.48., ...), custom_call_target="tpu_custom_call" | custom-call | tf_op jit(solution)/shard_map/ffn/pallas_call | solution.py:831
  180.9 103.8 %attn_bwd_reduce.1 = (bf16[48,5504]{1,0:T(8,128)(2,1)}, bf16[6,256,768]{2,1,0:T(8,128)(2,1)}) custom-call(f32[8,1536]{1,0:T(8,128)} %get-tuple-element.57.lse, s32[1,1536]{1,0:T(1,128)} %get-tuple-element.58.start, bf16[4,1536,128]{2,1,0:T(8,128)(2,1)} %get-tuple-element.59.q_i, bf16[4,1536,128]{2,1,0:T(8,128)(2,1)} %get-tuple-element.60.k_i, ...), custom_call_target="tpu_custom_call" | custom-call | tf_op jit(solution)/shard_map/attn_bwd_reduce/pallas_call | solution.py:654
  284.8 5.9 %finish.1 = (f32[6,256,768]{2,1,0:T(8,128)}, f32[48,1280]{1,0:T(8,128)}, f32[48,1280]{1,0:T(8,128)}, f32[48,1280]{1,0:T(8,128)}, f32[48,384]{1,0:T(8,128)}, /*in...) custom-call(bf16[6,256,768]{2,1,0:T(8,128)(2,1)} %get-tuple-element.74.gtok, ...), custom_call_target="tpu_custom_call" | custom-call | tf_op jit(solution)/shard_map/finish/pallas_call | solution.py:951
  290.6 1.3 slice_bitcast_fusion
  291.9 3.2 %copy.25 = bf16[1536,768]{1,0:T(8,128)(2,1)} copy(bf16[1536,768]{1,0:T(8,128)(2,1)} %bitcast.20) | data formatting | bytes 4718592
